TPU v7x, 32 devices: a whole 2x2x4 slice. The times are simulated.
32 devices in a mesh: dp: 16 (over z, x, core), tensor: 2 (over y).
Axes of the slice: x: 2, y: 2, z: 4, core: 2. Of those that a mesh axis runs over, the one named last changes fastest.
Arguments:
- content_in: bfloat16 [32, 512, 768], P('dp'), may hold values from -6 to 6
- query_in: bfloat16 [32, 512, 768], P('dp'), may hold values from -6 to 6
- lengths: int32 [32], P('dp'), may hold values from 1 to 512, 9830 in all
- factor_order: int32 [32, 512], P('dp'), may hold values from 0 to 511, each once within a row
- buckets: int32 [32, 512, 512], P('dp'), may hold values from 0 to 31
- w_qkv: bfloat16 [3, 768, 768], P(None, 'dp', 'tensor'), may hold values from -0.21875 to 0.21875
- b_qv: bfloat16 [2, 768], P(None, 'tensor'), may hold values from -3 to 3
- w_out: bfloat16 [768, 768], P('tensor', 'dp'), may hold values from -1.75 to 1.75
- w_in: bfloat16 [768, 3072], P('dp', 'tensor'), may hold values from -0.21875 to 0.21875
- b_in: bfloat16 [3072], P('tensor'), may hold values from -3 to 3
- w_down: bfloat16 [3072, 768], P('tensor', 'dp'), may hold values from -0.109375 to 0.109375
- b_outs: bfloat16 [2, 768], replicated, may hold values from -2 to 2
- norm_gain: bfloat16 [2, 768], replicated, may hold values from 0.5 to 1.5
- norm_bias: bfloat16 [2, 768], replicated, may hold values from -2 to 2
- rel_table: bfloat16 [32, 12], P(None, 'tensor'), may hold values from -4 to 4
- cot_content: bfloat16 [32, 512, 768], P('dp'), may hold values from -6 to 6
- cot_query: bfloat16 [32, 512, 768], P('dp'), may hold values from -6 to 6
Outputs:
- out_content: bfloat16 [32, 512, 768], P('dp')
- out_query: bfloat16 [32, 512, 768], P('dp')
- grad_content: bfloat16 [32, 512, 768], P('dp', None, 'tensor')
- grad_query: bfloat16 [32, 512, 768], P('dp', None, 'tensor')
- grad_w_qkv: float32 [3, 768, 768], P(None, 'dp', 'tensor')
- grad_b_qv: float32 [2, 768], P(None, 'tensor')
- grad_w_out: float32 [768, 768], P('tensor', 'dp')
- grad_w_in: float32 [768, 3072], P('dp', 'tensor')
- grad_b_in: float32 [3072], P('tensor')
- grad_w_down: float32 [3072, 768], P('tensor', 'dp')
- grad_b_outs: float32 [2, 768], replicated
- grad_norm_gain: float32 [2, 768], replicated
- grad_norm_bias: float32 [2, 768], replicated
- grad_rel_table: float32 [32, 12], P(None, 'tensor')
Inputs may be any that keep to these rules, and one draw needn't show every extreme that they name: `lengths`: positions at or past a sequence's length are padding; some sequence uses all 512 slots. `factor_order`: each row is a permutation of the positions 0 to 511.
All inputs are finite; a program needn't handle non-finite values. No bound on the sum of `lengths` on one device may be relied on, other than what follows from the above.
Results may differ from a plain program's by a relative error of at most 0.019.
Values may be sent and summed in bfloat16 or wider, within the bound.
No kernel may reach another device: no remote copies, remote signals or barrier semaphores. Data moves between devices by JAX's collectives and lax.ppermute only.
A program may use at most 256 MiB of HBM per device.

v0:
```python
import jax
import jax.numpy as jnp
from jax import lax
from jax.sharding import PartitionSpec as P

MB = 2


EPSILON = 1e-05
PRECISE = lax.Precision.HIGHEST
MASKED = -1e30


def layer_norm(residual, gain_row, shift_row):
    average = jnp.mean(residual, axis=-1, keepdims=True)
    centred = residual - average
    variance = jnp.mean(centred * centred, axis=-1, keepdims=True)
    return centred * lax.rsqrt(variance + EPSILON) * gain_row + shift_row


def gelu_exact(values):
    return 0.5 * values * (1.0 + lax.erf(values * 0.7071067811865476))


def visibility(lengths, factor_order, seq_len):
    positions = jnp.arange(seq_len, dtype=jnp.int32)
    key_valid = positions[None, None, :] < lengths[:, None, None]
    rank_query = factor_order[:, :, None]
    rank_key = factor_order[:, None, :]
    itself = (positions[:, None] == positions[None, :])[None]
    content_mask = key_valid & (rank_key <= rank_query) | itself
    query_mask = key_valid & (rank_key < rank_query) | (positions[None, None, :] == 0)
    return (content_mask, query_mask)


def masked_scores(query_heads, key_heads, visible, pair_bias):
    raw_scores = (
        jnp.einsum("rihd,rjhd->rhij", query_heads, key_heads, preferred_element_type=jnp.float32)
        * 0.125
    )
    return jnp.where(visible[:, None], raw_scores + pair_bias, MASKED)


def attend(query_heads, key_heads, value_heads, visible, pair_bias):
    scores = masked_scores(query_heads, key_heads, visible, pair_bias)
    row_max = jnp.max(scores, axis=-1, keepdims=True)
    exp_scores = jnp.exp(scores - row_max)
    row_sum = jnp.sum(exp_scores, axis=-1, keepdims=True)
    attn_low = (exp_scores / row_sum).astype(jnp.bfloat16)
    context = jnp.einsum(
        "rhij,rjhd->rihd", attn_low, value_heads, preferred_element_type=jnp.float32
    )
    return (context.astype(jnp.bfloat16), row_max + jnp.log(row_sum))


def attend_back(query_heads, key_heads, value_heads, visible, pair_bias, log_total, context_grad):
    scores = masked_scores(query_heads, key_heads, visible, pair_bias)
    attn = jnp.exp(scores - log_total)
    attn_low = attn.astype(jnp.bfloat16)
    value_grad = jnp.einsum(
        "rhij,rihd->rjhd", attn_low, context_grad, preferred_element_type=jnp.float32
    )
    attn_grad = jnp.einsum(
        "rihd,rjhd->rhij", context_grad, value_heads, preferred_element_type=jnp.float32
    )
    inner = jnp.sum(attn * attn_grad, axis=-1, keepdims=True)
    score_grad = attn * (attn_grad - inner)
    score_low = score_grad.astype(jnp.bfloat16)
    query_grad = (
        jnp.einsum("rhij,rjhd->rihd", score_low, key_heads, preferred_element_type=jnp.float32)
        * 0.125
    )
    key_grad = (
        jnp.einsum("rhij,rihd->rjhd", score_low, query_heads, preferred_element_type=jnp.float32)
        * 0.125
    )
    return (query_grad, key_grad, value_grad, score_grad)


def shards(
    content_in,
    query_in,
    lengths,
    factor_order,
    buckets,
    w_qkv,
    b_qv,
    w_out,
    w_in,
    b_in,
    w_down,
    b_outs,
    norm_gain,
    norm_bias,
    rel_table,
    cot_content,
    cot_query,
):
    seq_rows = content_in.shape[0] // MB
    seq_len = content_in.shape[1]
    width = content_in.shape[2]
    heads_here = rel_table.shape[1]
    bucket_count = rel_table.shape[0]
    attn_width = w_qkv.shape[2]
    ffn_width = w_in.shape[1]
    head_size = attn_width // heads_here
    tokens = seq_rows * seq_len
    half_width = width // lax.axis_size("tensor")
    column_start = lax.axis_index("tensor") * half_width
    head_shape = (seq_rows, seq_len, heads_here, head_size)
    sharded = (w_qkv, w_out, w_in, w_down)
    gains = norm_gain.astype(jnp.float32)
    shifts = norm_bias.astype(jnp.float32)
    out_bias = b_outs.astype(jnp.float32)
    qv_bias = b_qv.astype(jnp.float32)
    inner_bias = b_in.astype(jnp.float32)
    table = rel_table.astype(jnp.float32)
    grad_shards = tuple((jnp.zeros(w.shape, jnp.float32) for w in sharded))
    small_sums = (
        jnp.zeros((2, attn_width), jnp.float32),
        jnp.zeros((ffn_width,), jnp.float32),
        jnp.zeros((2, width), jnp.float32),
        jnp.zeros((2, width), jnp.float32),
        jnp.zeros((2, width), jnp.float32),
        jnp.zeros((bucket_count, heads_here), jnp.float32),
    )
    content_outs = []
    query_outs = []
    content_grads = []
    query_grads = []
    for batch in range(MB):
        begin = batch * seq_rows
        full_qkv, full_out, full_in, full_down = (
            lax.all_gather(sharded[0], "dp", axis=1, tiled=True),
            lax.all_gather(sharded[1], "dp", axis=1, tiled=True),
            lax.all_gather(sharded[2], "dp", axis=0, tiled=True),
            lax.all_gather(sharded[3], "dp", axis=1, tiled=True),
        )
        content_flat = lax.slice_in_dim(content_in, begin, begin + seq_rows, axis=0).reshape(
            tokens, width
        )
        query_flat = lax.slice_in_dim(query_in, begin, begin + seq_rows, axis=0).reshape(
            tokens, width
        )
        length_rows = lax.slice_in_dim(lengths, begin, begin + seq_rows, axis=0)
        order_rows = lax.slice_in_dim(factor_order, begin, begin + seq_rows, axis=0)
        bucket_rows = lax.slice_in_dim(buckets, begin, begin + seq_rows, axis=0)
        stacked = jnp.concatenate([content_flat, query_flat], axis=0)
        query_low = (
            jnp.dot(stacked, full_qkv[0], preferred_element_type=jnp.float32) + qv_bias[0]
        ).astype(jnp.bfloat16)
        key_value = jnp.einsum(
            "nd,tde->tne", content_flat, full_qkv[1:], preferred_element_type=jnp.float32
        )
        key_heads = key_value[0].astype(jnp.bfloat16).reshape(head_shape)
        value_heads = (key_value[1] + qv_bias[1]).astype(jnp.bfloat16).reshape(head_shape)
        query_content = query_low[:tokens].reshape(head_shape)
        query_stream = query_low[tokens:].reshape(head_shape)
        content_mask, query_mask = visibility(length_rows, order_rows, seq_len)
        one_hot = (bucket_rows[..., None] == jnp.arange(bucket_count, dtype=jnp.int32)).astype(
            jnp.float32
        )
        pair_bias = jnp.einsum("rijn,nh->rhij", one_hot, table, precision=PRECISE)
        context_content, log_content = attend(
            query_content, key_heads, value_heads, content_mask, pair_bias
        )
        context_query, log_query = attend(
            query_stream, key_heads, value_heads, query_mask, pair_bias
        )
        context_both = jnp.concatenate(
            [
                context_content.reshape(tokens, attn_width),
                context_query.reshape(tokens, attn_width),
            ],
            axis=0,
        )
        attn_part = jnp.dot(context_both, full_out, preferred_element_type=jnp.float32)
        attn_share = lax.psum_scatter(
            attn_part.astype(jnp.bfloat16), "tensor", scatter_dimension=0, tiled=True
        ).astype(jnp.float32)
        attn_total = lax.all_gather(
            attn_share.astype(jnp.bfloat16), "tensor", axis=0, tiled=True
        ).astype(attn_share.dtype)
        residual_one = stacked.astype(jnp.float32) + attn_total + out_bias[0]
        normed, norm_one_back = jax.vjp(layer_norm, residual_one, gains[0], shifts[0])
        normed_low = normed.astype(jnp.bfloat16)
        hidden = jnp.dot(normed_low, full_in, preferred_element_type=jnp.float32) + inner_bias
        active, gelu_back = jax.vjp(gelu_exact, hidden)
        active_low = active.astype(jnp.bfloat16)
        ffn_part = jnp.dot(active_low, full_down, preferred_element_type=jnp.float32)
        ffn_share = lax.psum_scatter(
            ffn_part.astype(jnp.bfloat16), "tensor", scatter_dimension=0, tiled=True
        ).astype(jnp.float32)
        ffn_total = lax.all_gather(
            ffn_share.astype(jnp.bfloat16), "tensor", axis=0, tiled=True
        ).astype(ffn_share.dtype)
        residual_two = normed + ffn_total + out_bias[1]
        output, norm_two_back = jax.vjp(layer_norm, residual_two, gains[1], shifts[1])
        output_low = output.astype(jnp.bfloat16)
        content_outs.append(output_low[:tokens].reshape(seq_rows, seq_len, width))
        query_outs.append(output_low[tokens:].reshape(seq_rows, seq_len, width))
        full_qkv, full_out, full_in, full_down = (
            lax.all_gather(sharded[0], "dp", axis=1, tiled=True),
            lax.all_gather(sharded[1], "dp", axis=1, tiled=True),
            lax.all_gather(sharded[2], "dp", axis=0, tiled=True),
            lax.all_gather(sharded[3], "dp", axis=1, tiled=True),
        )
        cotangent = jnp.concatenate(
            [
                lax.slice_in_dim(cot_content, begin, begin + seq_rows, axis=0).reshape(
                    tokens, width
                ),
                lax.slice_in_dim(cot_query, begin, begin + seq_rows, axis=0).reshape(tokens, width),
            ],
            axis=0,
        ).astype(jnp.float32)
        resid_two_grad, gain_two, shift_two = norm_two_back(cotangent)
        ffn_out_low = resid_two_grad.astype(jnp.bfloat16)
        active_grad = jnp.dot(ffn_out_low, full_down.T, preferred_element_type=jnp.float32)
        down_grad = jnp.dot(active_low.T, ffn_out_low, preferred_element_type=jnp.float32)
        (hidden_grad,) = gelu_back(active_grad)
        hidden_low = hidden_grad.astype(jnp.bfloat16)
        in_grad = jnp.dot(normed_low.T, hidden_low, preferred_element_type=jnp.float32)
        normed_part = jnp.dot(hidden_low, full_in.T, preferred_element_type=jnp.float32)
        normed_share = lax.psum_scatter(
            normed_part.astype(jnp.bfloat16), "tensor", scatter_dimension=0, tiled=True
        ).astype(jnp.float32)
        normed_total = lax.all_gather(
            normed_share.astype(jnp.bfloat16), "tensor", axis=0, tiled=True
        ).astype(normed_share.dtype)
        resid_one_grad, gain_one, shift_one = norm_one_back(resid_two_grad + normed_total)
        attn_out_low = resid_one_grad.astype(jnp.bfloat16)
        out_grad = jnp.dot(context_both.T, attn_out_low, preferred_element_type=jnp.float32)
        context_grad = jnp.dot(attn_out_low, full_out.T, preferred_element_type=jnp.float32).astype(
            jnp.bfloat16
        )
        dq_content, dk_content, dv_content, ds_content = attend_back(
            query_content,
            key_heads,
            value_heads,
            content_mask,
            pair_bias,
            log_content,
            context_grad[:tokens].reshape(head_shape),
        )
        dq_query, dk_query, dv_query, ds_query = attend_back(
            query_stream,
            key_heads,
            value_heads,
            query_mask,
            pair_bias,
            log_query,
            context_grad[tokens:].reshape(head_shape),
        )
        table_grad = jnp.einsum("rhij,rijn->nh", ds_content + ds_query, one_hot, precision=PRECISE)
        query_grad = jnp.concatenate(
            [dq_content.reshape(tokens, attn_width), dq_query.reshape(tokens, attn_width)], axis=0
        )
        kv_grad = jnp.stack(
            [
                (dk_content + dk_query).reshape(tokens, attn_width),
                (dv_content + dv_query).reshape(tokens, attn_width),
            ]
        )
        query_grad_low = query_grad.astype(jnp.bfloat16)
        kv_grad_low = kv_grad.astype(jnp.bfloat16)
        qkv_grad = jnp.concatenate(
            [
                jnp.dot(stacked.T, query_grad_low, preferred_element_type=jnp.float32)[None],
                jnp.einsum(
                    "nd,tne->tde", content_flat, kv_grad_low, preferred_element_type=jnp.float32
                ),
            ],
            axis=0,
        )
        input_part = jnp.dot(query_grad_low, full_qkv[0].T, preferred_element_type=jnp.float32)
        content_extra = jnp.einsum(
            "tne,tde->nd", kv_grad_low, full_qkv[1:], preferred_element_type=jnp.float32
        )
        input_part = input_part.at[:tokens].add(content_extra)
        input_share = lax.psum_scatter(
            input_part.astype(jnp.bfloat16), "tensor", scatter_dimension=1, tiled=True
        ).astype(jnp.float32)
        residual_share = lax.dynamic_slice_in_dim(resid_one_grad, column_start, half_width, 1)
        input_grad = (residual_share + input_share).astype(jnp.bfloat16)
        content_grads.append(input_grad[:tokens].reshape(seq_rows, seq_len, half_width))
        query_grads.append(input_grad[tokens:].reshape(seq_rows, seq_len, half_width))
        step_grads = (qkv_grad, out_grad, in_grad, down_grad)
        shares = (
            lax.psum_scatter(step_grads[0], "dp", scatter_dimension=1, tiled=True),
            lax.psum_scatter(step_grads[1], "dp", scatter_dimension=1, tiled=True),
            lax.psum_scatter(step_grads[2], "dp", scatter_dimension=0, tiled=True),
            lax.psum_scatter(step_grads[3], "dp", scatter_dimension=1, tiled=True),
        )
        grad_shards = tuple((a + b for a, b in zip(grad_shards, shares)))
        step_small = (
            jnp.stack([jnp.sum(query_grad, axis=0), jnp.sum(kv_grad[1], axis=0)]),
            jnp.sum(hidden_grad, axis=0),
            jnp.stack([jnp.sum(resid_one_grad, axis=0), jnp.sum(resid_two_grad, axis=0)]),
            jnp.stack([gain_one, gain_two]),
            jnp.stack([shift_one, shift_two]),
            table_grad,
        )
        small_sums = tuple((a + b for a, b in zip(small_sums, step_small)))
    small_totals = lax.psum(small_sums, "dp")
    return (
        jnp.concatenate(content_outs, axis=0),
        jnp.concatenate(query_outs, axis=0),
        jnp.concatenate(content_grads, axis=0),
        jnp.concatenate(query_grads, axis=0),
        grad_shards[0],
        small_totals[0],
        grad_shards[1],
        grad_shards[2],
        small_totals[1],
        grad_shards[3],
        small_totals[2],
        small_totals[3],
        small_totals[4],
        small_totals[5],
    )


def solution(mesh):
    return jax.shard_map(
        shards,
        mesh=mesh,
        in_specs=(
            P("dp", None, None),
            P("dp", None, None),
            P("dp"),
            P("dp", None),
            P("dp", None, None),
            P(None, "dp", "tensor"),
            P(None, "tensor"),
            P("tensor", "dp"),
            P("dp", "tensor"),
            P("tensor"),
            P("tensor", "dp"),
            P(),
            P(),
            P(),
            P(None, "tensor"),
            P("dp", None, None),
            P("dp", None, None),
        ),
        out_specs=(
            P("dp", None, None),
            P("dp", None, None),
            P("dp", None, "tensor"),
            P("dp", None, "tensor"),
            P(None, "dp", "tensor"),
            P(None, "tensor"),
            P("tensor", "dp"),
            P("dp", "tensor"),
            P("tensor"),
            P("tensor", "dp"),
            P(),
            P(),
            P(),
            P(None, "tensor"),
        ),
        check_vma=False,
    )
```

profile of v0, /device:TPU:0, one launch (start us, length us, event | category | flops | bytes accessed | tf_op | source)
XLA Modules:
  0.0 1101.8 jit_solution(8611137368941104728)
XLA Ops:
  10.5 7.3 fusion.1
  17.8 9.1 copy.67
  26.9 7.2 fusion.3
  34.1 8.9 copy.64
  45.0 26.3 %all_gather.21 = bf16[384,768]{0,1:T(8,128)(2,1)} all-gather(bf16[384,48]{0,1:T(8,128)(2,1)S(1)} %copy-done.115), channel_id=1, replica_groups=mesh['dp'=16,'tensor'=2] {'dp'}, dimensions={1}, use_global_device_ids=true | all-gather | bytes 626688 | tf_op jit(solution)/shard_map/all_gather | solution.py:135
  95.7 4.4 fusion.162
  111.4 7.5 reduce-scatter.20.cloned.1.call-done
  119.1 28.9 %reduce-scatter.16.cloned.1.call-done = bf16[512,768]{1,0:T(8,128)(2,1)} async-done(((bf16[1024,768]{1,0:T(8,128)(2,1)}), bf16[512,768]{1,0:T(8,128)(2,1)}) %reduce-scatter.16.cloned.1.call-update) | async-done | bytes 786448 | tf_op jit(solution)/shard_map/reduce_scatter | solution.py:178
  151.5 25.1 %all-gather.20.cloned.1.call-done = bf16[1024,768]{1,0:T(8,128)(2,1)} async-done(((bf16[512,768]{1,0:T(8,128)(2,1)}), bf16[1024,768]{1,0:T(8,128)(2,1)}) %all-gather.20.cloned.1.call-update) | async-done | bytes 1572880 | tf_op jit(solution)/shard_map/all_gather | solution.py:181
  176.6 28.6 %all-gather.12.cloned.1.call-done = bf16[1024,768]{1,0:T(8,128)(2,1)} async-done(((bf16[512,768]{1,0:T(8,128)(2,1)}), bf16[1024,768]{1,0:T(8,128)(2,1)}) %all-gather.12.cloned.1.call-update) | async-done | bytes 1572880 | tf_op jit(solution)/shard_map/all_gather | solution.py:181
  205.3 4.2 fusion.45
  211.5 38.3 %all-gather.14.cloned.1.call-done = bf16[768,1536]{1,0:T(8,128)(2,1)} async-done(((bf16[48,1536]{1,0:T(8,128)(2,1)}), bf16[768,1536]{1,0:T(8,128)(2,1)}) %all-gather.14.cloned.1.call-update) | async-done | bytes 2359312 | tf_op jit(solution)/shard_map/all_gather | solution.py:136
  249.8 8.3 multiply_convert_fusion
  258.1 35.1 %all-gather.16.cloned.1.call-done = bf16[1536,768]{0,1:T(8,128)(2,1)} async-done(((bf16[1536,48]{0,1:T(8,128)(2,1)}), bf16[1536,768]{0,1:T(8,128)(2,1)}) %all-gather.16.cloned.1.call-update) | async-done | bytes 2359312 | tf_op jit(solution)/shard_map/all_gather | solution.py:137
  293.2 6.4 convolution_convert_fusion.4
  299.7 25.0 %reduce-scatter.22.cloned.1.call-done = bf16[512,768]{1,0:T(8,128)(2,1)} async-done(((bf16[1024,768]{1,0:T(8,128)(2,1)}), bf16[512,768]{1,0:T(8,128)(2,1)}) %reduce-scatter.22.cloned.1.call-update) | async-done | bytes 786448 | tf_op jit(solution)/shard_map/reduce_scatter | solution.py:191
  328.3 25.2 %all-gather.22.cloned.1.call-done = bf16[1024,768]{1,0:T(8,128)(2,1)} async-done(((bf16[512,768]{1,0:T(8,128)(2,1)}), bf16[1024,768]{1,0:T(8,128)(2,1)}) %all-gather.22.cloned.1.call-update) | async-done | bytes 1572880 | tf_op jit(solution)/shard_map/all_gather | solution.py:194
  365.2 5.9 fusion.167
  376.5 26.2 %reduce-scatter.26.cloned.1.call-done = bf16[512,768]{1,0:T(8,128)(2,1)} async-done(((bf16[1024,768]{1,0:T(8,128)(2,1)}), bf16[512,768]{1,0:T(8,128)(2,1)}) %reduce-scatter.26.cloned.1.call-update) | async-done | bytes 786448 | tf_op jit(solution)/shard_map/reduce_scatter | solution.py:225
  403.8 27.6 %all-gather.26.cloned.1.call-done = bf16[1024,768]{1,0:T(8,128)(2,1)} async-done(((bf16[512,768]{1,0:T(8,128)(2,1)}), bf16[1024,768]{1,0:T(8,128)(2,1)}) %all-gather.26.cloned.1.call-update) | async-done | bytes 1572880 | tf_op jit(solution)/shard_map/all_gather | solution.py:228
  431.5 7.8 fusion.142
  439.4 6.2 multiply_convert_fusion.1
  451.0 26.2 %reduce-scatter.18.cloned.1.call-done = bf16[512,768]{1,0:T(8,128)(2,1)} async-done(((bf16[1024,768]{1,0:T(8,128)(2,1)}), bf16[512,768]{1,0:T(8,128)(2,1)}) %reduce-scatter.18.cloned.1.call-update) | async-done | bytes 786448 | tf_op jit(solution)/shard_map/reduce_scatter | solution.py:191
  477.2 28.8 %all-gather.18.cloned.1.call-done = bf16[1024,768]{1,0:T(8,128)(2,1)} async-done(((bf16[512,768]{1,0:T(8,128)(2,1)}), bf16[1024,768]{1,0:T(8,128)(2,1)}) %all-gather.18.cloned.1.call-update) | async-done | bytes 1572880 | tf_op jit(solution)/shard_map/all_gather | solution.py:194
  517.5 5.9 fusion.166
  528.9 26.2 %reduce-scatter.24.cloned.1.call-done = bf16[512,768]{1,0:T(8,128)(2,1)} async-done(((bf16[1024,768]{1,0:T(8,128)(2,1)}), bf16[512,768]{1,0:T(8,128)(2,1)}) %reduce-scatter.24.cloned.1.call-update) | async-done | bytes 786448 | tf_op jit(solution)/shard_map/reduce_scatter | solution.py:225
  562.0 21.7 %all-gather.24.cloned.1.call-done = bf16[1024,768]{1,0:T(8,128)(2,1)} async-done(((bf16[512,768]{1,0:T(8,128)(2,1)}), bf16[1024,768]{1,0:T(8,128)(2,1)}) %all-gather.24.cloned.1.call-update) | async-done | bytes 1572880 | tf_op jit(solution)/shard_map/all_gather | solution.py:228
  583.7 8.1 fusion.143
  595.5 5.6 fusion.145
  612.8 9.0 fusion.50
  636.7 4.1 multiply_reduce_fusion.1
  640.8 8.9 fusion.53
  660.1 5.5 fusion.155
  667.5 4.1 fusion.153
  693.8 6.3 copy.92
  721.3 6.0 fusion.127
  727.3 4.7 convolution_add_fusion
  732.6 5.7 fusion.60
  738.3 5.3 convolution_add_fusion.1
  749.0 9.9 copy.93
  759.0 9.8 copy.94
  768.9 18.6 %fusion.87 = f32[32,6]{0,1:T(8,128)S(1)} fusion(f32[6,512,512]{2,0,1:T(8,128)} %copy.93, s32[512,512]{1,0:T(8,128)S(1)} %copy-done.40), kind=kOutput, calls=%fused_computation.177 | convolution fusion | flops 612368384 | bytes 7340800 | tf_op jit(solution)/shard_map/rhij,rijn->nh/dot_general | solution.py:255
  787.5 16.3 %fusion.89 = f32[32,6]{0,1:T(8,128)S(1)} fusion(f32[32,6]{0,1:T(8,128)S(1)} %fusion.87, f32[6,512,512]{2,0,1:T(8,128)S(1)} %copy-done.36, s32[512,512]{1,0:T(8,128)S(1)} %copy-done.38), kind=kOutput, calls=%fused_computation.179 | convolution fusion | flops 612368576 | bytes 7341568 | tf_op jit(solution)/shard_map/rhij,rijn->nh/dot_general | solution.py:255
  803.8 61.6 %all-reduce.1 = (f32[2,384]{1,0:T(2,128)}, f32[1536]{0:T(1024)}, f32[2,768]{1,0:T(2,128)}, f32[2,768]{1,0:T(2,128)}, f32[2,768]{1,0:T(2,128)}, /*index=5*/f32[32,6]{0,1:T(8,128)}) all-reduce(f32[2,384]{1,0:T(2,128)S(1)} %maximum_add_fusion.4, f32[1536]{0:T(1024)S(1)} %add.448, ...), channel_id=1, replica_groups=mesh['dp'=16,'tensor'=2] {'dp'}, use_global_device_ids=true, to_apply=%region_44.45 | all-reduce | flops 7104 | bytes 56832 | tf_op jit(solution)/shard_map/psum | solution.py:305
  868.6 5.0 reduce-scatter.36.cloned.1.call-done
  879.8 56.2 %reduce-scatter.28.cloned.1.call-done = f32[384,48]{0,1:T(8,128)} async-done(((f32[384,768]{0,1:T(8,128)}), f32[384,48]{0,1:T(8,128)}) %reduce-scatter.28.cloned.1.call-update) | async-done | bytes 73744 | tf_op jit(solution)/shard_map/reduce_scatter | solution.py:291
  936.0 78.8 %reduce-scatter.32.cloned.1.call-done = f32[1536,48]{0,1:T(8,128)} async-done(((f32[1536,768]{0,1:T(8,128)}), f32[1536,48]{0,1:T(8,128)}) %reduce-scatter.32.cloned.1.call-update) | async-done | bytes 294928 | tf_op jit(solution)/shard_map/reduce_scatter | solution.py:293
  1014.8 79.6 %reduce-scatter.30.cloned.1.call-done = f32[48,1536]{1,0:T(8,128)} async-done(((f32[768,1536]{1,0:T(8,128)}), f32[48,1536]{1,0:T(8,128)}) %reduce-scatter.30.cloned.1.call-update) | async-done | bytes 294928 | tf_op jit(solution)/shard_map/reduce_scatter | solution.py:292
  (562 shorter events, 196.6 us)
Async XLA Ops:
  7.2 68.6 %all-gather.10.cloned.1.call-start = ((), (), s32[]{:S(2)}) async-start(), calls=%async_computation.11 | async-start | bytes 1880064 | tf_op jit(solution)/shard_map/all_gather | solution.py:134
  7.9 111.0 %reduce-scatter.20.cloned.1.call-start = ((), (), s32[]{:S(2)}) async-start(), calls=%async_computation.18 | async-start | bytes 2359296 | tf_op jit(solution)/shard_map/reduce_scatter | solution.py:178
  10.5 16.4 %copy-start.39 = (s32[512,512]{1,0:T(8,128)}, s32[512,512]{1,0:T(8,128)S(1)}, u32[]{:S(2)}) copy-start(s32[512,512]{1,0:T(8,128)S(1)} %get-tuple-element.124) | copy-start | bytes 3145732
  34.1 9.0 copy-start.150
  34.1 10.9 copy-start.146
  34.1 10.9 copy-start.115
  73.4 280.1 %copy-start.12 = (bf16[512,768]{1,0:T(8,128)(2,1)}, bf16[512,768]{1,0:T(8,128)(2,1)S(1)}, u32[]{:S(2)}) copy-start(bf16[512,768]{1,0:T(8,128)(2,1)S(1)} %get-tuple-element.135) | copy-start | bytes 2359300
  73.4 280.1 %copy-start.16 = (bf16[512,768]{1,0:T(8,128)(2,1)}, bf16[512,768]{1,0:T(8,128)(2,1)S(1)}, u32[]{:S(2)}) copy-start(bf16[512,768]{1,0:T(8,128)(2,1)S(1)} %get-tuple-element.204) | copy-start | bytes 2359300
  79.5 546.3 %copy-start.35 = (bf16[1,512,384]{1,2,0:T(8,128)(2,1)}, bf16[1,512,384]{1,2,0:T(8,128)(2,1)S(1)}, u32[]{:S(2)}) copy-start(bf16[1,512,384]{1,2,0:T(8,128)(2,1)S(1)} %slice.330) | copy-start | bytes 1179652
  90.0 17.2 %copy-start.51 = (bf16[512,6,64]{0,2,1:T(8,128)(2,1)}, bf16[512,6,64]{0,2,1:T(8,128)(2,1)S(1)}, u32[]{:S(2)}) copy-start(bf16[512,6,64]{0,2,1:T(8,128)(2,1)S(1)} %get-tuple-element.166) | copy-start | bytes 1179652
  95.4 52.6 %reduce-scatter.16.cloned.1.call-start = ((), (), s32[]{:S(2)}) async-start(), calls=%async_computation.12 | async-start | bytes 2359296 | tf_op jit(solution)/shard_map/reduce_scatter | solution.py:178
  109.2 40.4 %copy-start.147 = (bf16[2,768]{1,0:T(2,128)(2,1)S(1)}, bf16[2,768]{1,0:T(2,128)(2,1)}, u32[]{:S(2)}) copy-start(bf16[2,768]{1,0:T(2,128)(2,1)} %param.32) | copy-start | bytes 9220
  109.2 40.4 %copy-start.148 = (bf16[2,768]{1,0:T(2,128)(2,1)S(1)}, bf16[2,768]{1,0:T(2,128)(2,1)}, u32[]{:S(2)}) copy-start(bf16[2,768]{1,0:T(2,128)(2,1)} %param.33) | copy-start | bytes 9220
  109.2 40.4 %copy-start.149 = (bf16[2,768]{1,0:T(2,128)(2,1)S(1)}, bf16[2,768]{1,0:T(2,128)(2,1)}, u32[]{:S(2)}) copy-start(bf16[2,768]{1,0:T(2,128)(2,1)} %param.34) | copy-start | bytes 9220
  109.2 40.5 %copy-start.145 = (bf16[1536]{0:T(1024)(128)(2,1)S(1)}, bf16[1536]{0:T(1024)(128)(2,1)}, u32[]{:S(2)}) copy-start(bf16[1536]{0:T(1024)(128)(2,1)} %param.30) | copy-start | bytes 9220
  111.4 65.2 %all-gather.20.cloned.1.call-start = ((), (), s32[]{:S(2)}) async-start(), calls=%async_computation.19 | async-start | bytes 2359296 | tf_op jit(solution)/shard_map/all_gather | solution.py:181
  119.0 86.3 %all-gather.12.cloned.1.call-start = ((), (), s32[]{:S(2)}) async-start(), calls=%async_computation.13 | async-start | bytes 2359296 | tf_op jit(solution)/shard_map/all_gather | solution.py:181
  148.0 101.8 %all-gather.14.cloned.1.call-start = ((), (), s32[]{:S(2)}) async-start(), calls=%async_computation.14 | async-start | bytes 2506752 | tf_op jit(solution)/shard_map/all_gather | solution.py:136
  148.6 144.6 %all-gather.16.cloned.1.call-start = ((), (), s32[]{:S(2)}) async-start(), calls=%async_computation.15 | async-start | bytes 2506752 | tf_op jit(solution)/shard_map/all_gather | solution.py:137
  149.3 175.3 %reduce-scatter.22.cloned.1.call-start = ((), (), s32[]{:S(2)}) async-start(), calls=%async_computation.20 | async-start | bytes 2359296 | tf_op jit(solution)/shard_map/reduce_scatter | solution.py:191
  151.5 210.4 %copy-start.99 = (f32[768]{0:T(1024)}, f32[768]{0:T(1024)S(1)}, u32[]{:S(2)}) copy-start(f32[768]{0:T(1024)S(1)} %get-tuple-element.208) | copy-start | bytes 9220
  299.6 53.9 %all-gather.22.cloned.1.call-start = ((), (), s32[]{:S(2)}) async-start(), calls=%async_computation.21 | async-start | bytes 2359296 | tf_op jit(solution)/shard_map/all_gather | solution.py:194
  324.6 78.0 %reduce-scatter.26.cloned.1.call-start = ((), (), s32[]{:S(2)}) async-start(), calls=%async_computation.24 | async-start | bytes 2359296 | tf_op jit(solution)/shard_map/reduce_scatter | solution.py:225
  353.5 11.6 %slice-start.14 = ((s8[6291456]{0:T(1024)(128)(4,1)}), s8[4194304]{0:T(1024)(128)(4,1)S(1)}, s32[]{:S(2)}) async-start(s8[6291456]{0:T(1024)(128)(4,1)} %bitcast.303), calls=%async_computation.46 | async-start | bytes 8388608
  376.4 55.0 %copy-start.7 = (bf16[1024,768]{1,0:T(8,128)(2,1)S(1)}, bf16[1024,768]{1,0:T(8,128)(2,1)}, u32[]{:S(2)}) copy-start(bf16[1024,768]{1,0:T(8,128)(2,1)} %all-gather.12.cloned.1.call-done) | copy-start | bytes 4718596
  376.5 55.0 %all-gather.26.cloned.1.call-start = ((), (), s32[]{:S(2)}) async-start(), calls=%async_computation.25 | async-start | bytes 2359296 | tf_op jit(solution)/shard_map/all_gather | solution.py:228
  402.7 74.4 %reduce-scatter.18.cloned.1.call-start = ((), (), s32[]{:S(2)}) async-start(), calls=%async_computation.16 | async-start | bytes 2359296 | tf_op jit(solution)/shard_map/reduce_scatter | solution.py:191
  450.9 55.1 %all-gather.18.cloned.1.call-start = ((), (), s32[]{:S(2)}) async-start(), calls=%async_computation.17 | async-start | bytes 2359296 | tf_op jit(solution)/shard_map/all_gather | solution.py:194
  477.1 77.9 %reduce-scatter.24.cloned.1.call-start = ((), (), s32[]{:S(2)}) async-start(), calls=%async_computation.22 | async-start | bytes 2359296 | tf_op jit(solution)/shard_map/reduce_scatter | solution.py:225
  506.0 11.5 %slice-start.16 = ((s8[6291456]{0:T(1024)(128)(4,1)}), s8[4194304]{0:T(1024)(128)(4,1)S(1)}, s32[]{:S(2)}) async-start(s8[6291456]{0:T(1024)(128)(4,1)} %bitcast.305), calls=%async_computation.48 | async-start | bytes 8388608
  528.8 54.9 %all-gather.24.cloned.1.call-start = ((), (), s32[]{:S(2)}) async-start(), calls=%async_computation.23 | async-start | bytes 2359296 | tf_op jit(solution)/shard_map/all_gather | solution.py:228
  555.1 310.3 %all-reduce.4.cloned.1.call-start = ((), (), s32[]{:S(2)}) async-start(), calls=%async_computation.31 | async-start | bytes 9437184
  583.7 8.2 copy-start.25
  583.7 8.2 copy-start.108
  612.8 9.0 copy-start.61
  621.8 8.9 slice-start.2
  640.8 8.9 copy-start.59
  700.1 167.0 %reduce-scatter.34.cloned.1.call-start = ((), (), s32[]{:S(2)}) async-start(), calls=%async_computation.29 | async-start | bytes 2359296
  707.9 165.8 %reduce-scatter.36.cloned.1.call-start = ((), (), s32[]{:S(2)}) async-start(), calls=%async_computation.30 | async-start | bytes 2359296
  715.7 220.3 %reduce-scatter.28.cloned.1.call-start = ((), (), s32[]{:S(2)}) async-start(), calls=%async_computation.26 | async-start | bytes 1253376 | tf_op jit(solution)/shard_map/reduce_scatter | solution.py:291
  721.2 293.6 %reduce-scatter.32.cloned.1.call-start = ((), (), s32[]{:S(2)}) async-start(), calls=%async_computation.28 | async-start | bytes 5013504 | tf_op jit(solution)/shard_map/reduce_scatter | solution.py:293
  732.0 362.4 %reduce-scatter.30.cloned.1.call-start = ((), (), s32[]{:S(2)}) async-start(), calls=%async_computation.27 | async-start | bytes 5013504 | tf_op jit(solution)/shard_map/reduce_scatter | solution.py:292
  749.0 9.9 copy-start.122
  749.0 9.9 copy-start.124
  759.0 9.9 copy-start.40
  768.9 18.6 %copy-start.36 = (f32[6,512,512]{2,0,1:T(8,128)S(1)}, f32[6,512,512]{2,0,1:T(8,128)}, u32[]{:S(2)}) copy-start(f32[6,512,512]{2,0,1:T(8,128)} %copy.94) | copy-start | bytes 18874372
  768.9 18.6 %copy-start.38 = (s32[512,512]{1,0:T(8,128)S(1)}, s32[512,512]{1,0:T(8,128)}, u32[]{:S(2)}) copy-start(s32[512,512]{1,0:T(8,128)} %copy-done.37) | copy-start | bytes 3145732
  877.5 216.9 %copy-start.1 = (bf16[32,6]{0,1:T(8,128)(2,1)S(1)}, bf16[32,6]{0,1:T(8,128)(2,1)}, u32[]{:S(2)}) copy-start(bf16[32,6]{0,1:T(8,128)(2,1)} %param.35) | copy-start | bytes 1156
  (154 other events, 568.8 us)
Sparse Core Ops, SparseCore 0:
  10.3 43.1 all-gather.9
  95.5 23.3 reduce-scatter.19
  121.9 26.0 reduce-scatter.15
  149.4 27.2 all-gather.19
  178.0 27.2 all-gather.11
  207.4 42.3 all-gather.13
  252.0 41.1 all-gather.15
  299.7 24.8 reduce-scatter.21
  326.2 27.1 all-gather.21
  376.6 26.0 reduce-scatter.25
  404.2 27.2 all-gather.25
  451.0 26.0 reduce-scatter.17
  478.7 27.2 all-gather.17
  529.0 26.0 reduce-scatter.23
  556.5 27.2 all-gather.23
  700.2 117.0 all-reduce.3
  819.5 25.8 reduce-scatter.33
  847.5 26.0 reduce-scatter.35
  877.9 58.1 reduce-scatter.27
  940.3 74.4 reduce-scatter.31
  1019.7 74.6 reduce-scatter.29
where the time goes:
time: 1110 us; the launch traced here: 1100 us
  waiting for transfers between devices  592 us (53%)
  matrix products  212 us (19%)
  other arithmetic  97.4 us (9%)
  local copies, waits for them, and re-layouts  91.7 us (8%)
  blocking collectives  87.9 us (8%)
  between operations  17.8 us (2%)
    reduce_scatter x1, waiting for transfers between devices, shards(): lax.psum_scatter(step_grads[2], 'dp', scatter_dimension=0, tiled=True)  79.6 us
    reduce_scatter x1, waiting for transfers between devices, shards(): lax.psum_scatter(step_grads[3], 'dp', scatter_dimension=1, tiled=True)  78.8 us
    psum x1, blocking collectives, shards(): small_totals = lax.psum(small_sums, 'dp')  61.6 us
    reduce_scatter x1, waiting for transfers between devices, shards(): lax.psum_scatter(step_grads[1], 'dp', scatter_dimension=1, tiled=True)  56.2 us
    all_gather x2, waiting for transfers between devices, shards(): lax.all_gather(ffn_share.astype(jnp.bfloat16), 'tensor', axis=0, tiled=True)  54 us
    all_gather x2, waiting for transfers between devices, shards(): lax.all_gather(attn_share.astype(jnp.bfloat16), 'tensor', axis=0, tiled=T...  53.8 us
    reduce_scatter x2, waiting for transfers between devices, shards(): lax.psum_scatter(normed_part.astype(jnp.bfloat16), 'tensor', scatter_dime...  52.3 us
    reduce_scatter x2, waiting for transfers between devices, shards(): lax.psum_scatter(ffn_part.astype(jnp.bfloat16), 'tensor', scatter_dimensi...  51.1 us
  transfers between devices with their start and end apart: 21, of which 18 were waited for; matrix products, arithmetic and copies ran while one was open for 17% of the time, Pallas kernels for 0%

commit v1 on v0

v1 whole, which is shorter than its diff:
```python
import functools

import jax
import jax.numpy as jnp
from jax import lax
from jax.experimental import pallas as pl
from jax.experimental.pallas import tpu as pltpu
from jax.sharding import Mesh, PartitionSpec as P

EPSILON = 1e-05

NEG = -1e30
BF = jnp.bfloat16
F32 = jnp.float32


def dot(a, b, dims):
    return lax.dot_general(a, b, (dims, ((), ())), preferred_element_type=F32)


NN = ((1,), (0,))
NT = ((1,), (1,))
TN = ((0,), (0,))


def bias_kernel(len_ref, buckets_ref, rank_row_ref, rank_col_ref, table_ref, out_ref):
    rows, cols = buckets_ref.shape
    heads = table_ref.shape[0]
    start = pl.program_id(0) * rows
    key = start + lax.broadcasted_iota(jnp.int32, (rows, cols), 0)
    query = lax.broadcasted_iota(jnp.int32, (rows, cols), 1)
    valid = key < len_ref[0]
    rank_key = rank_col_ref[...]
    rank_query = rank_row_ref[...]
    content = (valid & (rank_key <= rank_query)) | (key == query)
    stream = (valid & (rank_key < rank_query)) | (key == 0)
    index = buckets_ref[...]
    for head in range(heads):
        row = jnp.broadcast_to(table_ref[head : head + 1, :], (rows, 128))
        bias = jnp.concatenate(
            [
                jnp.take_along_axis(
                    row, index[:, c : c + 128], axis=1, mode="promise_in_bounds"
                )
                for c in range(0, cols, 128)
            ],
            axis=1,
        )
        out_ref[head, :, :cols] = jnp.where(content, bias, NEG).astype(BF)
        out_ref[head, :, cols:] = jnp.where(stream, bias, NEG).astype(BF)


def masked_bias(length, buckets_t, rank, table):
    seq = buckets_t.shape[0]
    heads = table.shape[0]
    step = 128
    return pl.pallas_call(
        bias_kernel,
        grid=(seq // step,),
        in_specs=[
            pl.BlockSpec(memory_space=pltpu.SMEM),
            pl.BlockSpec((step, seq), lambda g: (g, 0)),
            pl.BlockSpec((1, seq), lambda g: (0, 0)),
            pl.BlockSpec((step, 1), lambda g: (g, 0)),
            pl.BlockSpec((heads, 128), lambda g: (0, 0)),
        ],
        out_specs=pl.BlockSpec((heads, step, 2 * seq), lambda g: (0, g, 0)),
        out_shape=jax.ShapeDtypeStruct((heads, seq, 2 * seq), BF),
    )(length, buckets_t, rank.reshape(1, seq), rank.reshape(seq, 1), table)


def forward_kernel(q_ref, k_ref, v_ref, bias_ref, probs_ref, ctx_ref, inv_ref, *, tile):
    keys = (k_ref[...].astype(F32) * 0.125).astype(BF)
    values = v_ref[...]
    for t in range(q_ref.shape[1] // tile):
        at = pl.ds(t * tile, tile)
        scores = dot(keys, q_ref[:, at], TN) + bias_ref[0, :, at].astype(F32)
        high = jnp.max(scores, axis=0, keepdims=True)
        weight = jnp.exp(scores - high)
        inverse = 1.0 / jnp.sum(weight, axis=0, keepdims=True)
        low = weight.astype(BF)
        probs_ref[0, :, at] = low
        ctx_ref[:, at] = (dot(values, low, NN) * inverse).astype(BF)
        inv_ref[0, :, at] = inverse


def attention(q_t, k_t, v_t, bias, heads, tile=256):
    width, both = q_t.shape
    seq = k_t.shape[1]
    size = width // heads
    return pl.pallas_call(
        functools.partial(forward_kernel, tile=tile),
        grid=(heads,),
        in_specs=[
            pl.BlockSpec((size, both), lambda h: (h, 0)),
            pl.BlockSpec((size, seq), lambda h: (h, 0)),
            pl.BlockSpec((size, seq), lambda h: (h, 0)),
            pl.BlockSpec((1, seq, both), lambda h: (h, 0, 0)),
        ],
        out_specs=[
            pl.BlockSpec((1, seq, both), lambda h: (h, 0, 0)),
            pl.BlockSpec((size, both), lambda h: (h, 0)),
            pl.BlockSpec((1, 1, both), lambda h: (h, 0, 0)),
        ],
        out_shape=[
            jax.ShapeDtypeStruct((heads, seq, both), BF),
            jax.ShapeDtypeStruct((width, both), BF),
            jax.ShapeDtypeStruct((heads, 1, both), F32),
        ],
    )(q_t, k_t, v_t, bias)


def backward_kernel(
    q_ref, k_ref, v_ref, p_ref, inv_ref, ctx_ref, dctx_ref, buckets_ref,
    dq_ref, dk_ref, dv_ref, table_ref, held, total, *, tile, buckets,
):
    head = pl.program_id(0)
    heads = pl.num_programs(0)
    seq = k_ref.shape[1]
    group = 16
    queries = q_ref[...]
    keys = k_ref[...]
    values = v_ref[...]
    grad = dctx_ref[...].astype(F32) * inv_ref[0]
    inner = jnp.sum(grad * ctx_ref[...].astype(F32), axis=0, keepdims=True)
    grad = grad.astype(BF)
    dk = jnp.zeros(keys.shape, F32)
    dv = jnp.zeros(keys.shape, F32)
    for t in range(seq // tile):
        both = None
        for stream in range(2):
            lo = stream * seq + t * tile
            at = slice(lo, lo + tile)
            weight = p_ref[0, :, at]
            part = dot(values, grad[:, at], TN) - inner[:, at]
            ds = weight.astype(F32) * part
            low = ds.astype(BF)
            dv += dot(grad[:, at], weight, NT)
            dk += dot(queries[:, at], low, NT)
            dq_ref[:, at] = (dot(keys, low, NN) * 0.125).astype(BF)
            both = ds if both is None else both + ds
        both = both.astype(BF).reshape(seq // group, group, tile)
        held[:, pl.ds(pl.multiple_of(head * group, group), group), t * tile : (t + 1) * tile] = both
    dk_ref[...] = (dk * 0.125).astype(BF)
    dv_ref[...] = dv.astype(BF)

    @pl.when(head == heads - 1)
    def _():
        total[...] = jnp.zeros_like(total)

        @pl.loop(0, seq // group)
        def _(g):
            index = buckets_ref[pl.ds(pl.multiple_of(g * group, group), group), :]
            hot = jnp.concatenate(
                [jnp.where(index == n, 1.0, 0.0).astype(BF) for n in range(buckets)], axis=0
            )
            total[...] += dot(hot, held[g], NT)

        whole = total[...]
        row = lax.broadcasted_iota(jnp.int32, whole.shape, 0) % group
        col = lax.broadcasted_iota(jnp.int32, whole.shape, 1) % group
        kept = jnp.where(row == col, whole, 0.0)
        table_ref[...] = jnp.sum(kept.reshape(buckets, group, whole.shape[1]), axis=1)


def attention_back(q_t, k_t, v_t, probs, inverse, ctx_t, dctx_t, buckets_t, heads, buckets, tile=256):
    width, both = q_t.shape
    seq = k_t.shape[1]
    size = width // heads
    wide = pl.BlockSpec((size, both), lambda h: (h, 0))
    thin = pl.BlockSpec((size, seq), lambda h: (h, 0))
    return pl.pallas_call(
        functools.partial(backward_kernel, tile=tile, buckets=buckets),
        grid=(heads,),
        in_specs=[
            wide,
            thin,
            thin,
            pl.BlockSpec((1, seq, both), lambda h: (h, 0, 0)),
            pl.BlockSpec((1, 1, both), lambda h: (h, 0, 0)),
            wide,
            wide,
            pl.BlockSpec((seq, seq), lambda h: (0, 0)),
        ],
        out_specs=[wide, thin, thin, pl.BlockSpec((buckets, heads * 16), lambda h: (0, 0))],
        out_shape=[
            jax.ShapeDtypeStruct((width, both), BF),
            jax.ShapeDtypeStruct((width, seq), BF),
            jax.ShapeDtypeStruct((width, seq), BF),
            jax.ShapeDtypeStruct((buckets, heads * 16), F32),
        ],
        scratch_shapes=[
            pltpu.VMEM((seq // 16, heads * 16, seq), BF),
            pltpu.VMEM((buckets * 16, heads * 16), F32),
        ],
        compiler_params=pltpu.CompilerParams(vmem_limit_bytes=56 * 1024 * 1024),
    )(q_t, k_t, v_t, probs, inverse, ctx_t, dctx_t, buckets_t)


def shifted(value, axis, step):
    size = lax.axis_size(axis)
    return lax.ppermute(value, axis, [(i, (i + step) % size) for i in range(size)])


def gather_axis(value, axis, where):
    size = lax.axis_size(axis)
    me = lax.axis_index(axis)
    pieces = [value] + [shifted(value, axis, k) for k in range(1, size)]
    slots = []
    for j in range(size):
        which = lax.rem(me - j + size, size)
        chosen = pieces[0]
        for k in range(1, size):
            chosen = jnp.where(which == k, pieces[k], chosen)
        slots.append(chosen)
    return jnp.stack(slots, axis=where)


def gather_rows(shard, order):
    names = ["y", "z", "x", "core"]
    value, have = shard, []
    for axis in order:
        where = sum(names.index(a) < names.index(axis) for a in have)
        value = gather_axis(value, axis, where)
        have.append(axis)
    return value


def scatter_axis(value, axis, where, low=True):
    size = lax.axis_size(axis)
    me = lax.axis_index(axis)
    total = lax.dynamic_index_in_dim(value, me, where, keepdims=False).astype(F32)
    for k in range(1, size):
        out = lax.dynamic_index_in_dim(value, lax.rem(me + k, size), where, keepdims=False)
        total = total + shifted(out.astype(BF), axis, k).astype(F32)
    return total.astype(BF) if low else total


def scatter_rows(value, order):
    have = ["y", "z", "x", "core"]
    for axis in order:
        where = have.index(axis)
        have.remove(axis)
        value = scatter_axis(value, axis, where, low=bool(have))
    return value


def sum_all(value):
    for axis in ("core", "x", "y", "z"):
        size = lax.axis_size(axis)
        value = value + sum(shifted(value, axis, k) for k in range(1, size))
    return value


def normalise(value):
    centred = value - jnp.mean(value, axis=-1, keepdims=True)
    inverse = lax.rsqrt(jnp.mean(centred * centred, axis=-1, keepdims=True) + EPSILON)
    return centred * inverse, inverse


def normalise_back(grad, unit, inverse):
    mean = jnp.mean(grad, axis=-1, keepdims=True)
    along = jnp.mean(grad * unit, axis=-1, keepdims=True)
    return (grad - mean - unit * along) * inverse


def ein(spec, a, b):
    return jnp.einsum(spec, a, b, preferred_element_type=F32)


def shards(
    content_in,
    query_in,
    lengths,
    factor_order,
    buckets,
    w_qkv,
    b_qv,
    w_out,
    w_in,
    b_in,
    w_down,
    b_outs,
    norm_gain,
    norm_bias,
    rel_table,
    cot_content,
    cot_query,
):
    me = lax.axis_index("y")
    halves = lax.axis_size("y")
    each = content_in.shape[0] // halves
    assert each == 1
    seq = content_in.shape[1]
    width = content_in.shape[2]
    bucket_count, heads_here = rel_table.shape
    heads = heads_here * halves
    part = w_qkv.shape[2]
    ffn = w_in.shape[1]
    rows = w_in.shape[0]

    def mine(array):
        return lax.dynamic_index_in_dim(array, me, 0, keepdims=False)

    qkv_shard = jnp.transpose(w_qkv, (1, 0, 2)).reshape(rows, 3 * part)
    cut = 5 * part // 3
    first = gather_rows(qkv_shard[:, :cut], ("z", "x", "y", "core"))
    second = gather_rows(qkv_shard[:, cut:], ("z", "y", "x", "core"))
    full_qkv = jnp.concatenate([first, second], axis=-1).reshape(halves, width, 3 * part)
    rest_shard = jnp.concatenate([w_in, w_down.T, w_out.T], axis=1)
    rest = lax.all_gather(rest_shard, ("y", "z", "x", "core"), axis=0).reshape(
        halves, width, 2 * ffn + part
    )
    w_q, w_k, w_v = (full_qkv[:, :, i * part : (i + 1) * part] for i in range(3))
    full_in, full_down, full_out = rest[:, :, :ffn], rest[:, :, ffn : 2 * ffn], rest[:, :, 2 * ffn :]

    vectors = jnp.concatenate([b_qv, b_in.reshape(ffn // part, part)], axis=0)
    vectors = jnp.concatenate(
        [vectors, jnp.pad(rel_table, ((0, 0), (0, part - heads_here)))], axis=0
    )
    vectors = gather_axis(vectors, "y", 0).astype(F32)
    q_bias = vectors[:, 0].reshape(width, 1)
    v_bias = vectors[:, 1].reshape(width, 1)
    hidden_bias = vectors[:, 2 : 2 + ffn // part].reshape(halves, 1, ffn)
    table = vectors[:, 2 + ffn // part :, :heads_here]
    table = jnp.transpose(table, (0, 2, 1)).reshape(heads, bucket_count)
    table = jnp.pad(table, ((0, 0), (0, 128 - bucket_count)))

    gains = norm_gain.astype(F32)
    shifts = norm_bias.astype(F32)
    out_bias = b_outs.astype(F32)

    content = mine(content_in)
    stacked = jnp.concatenate([content, mine(query_in)], axis=0)
    buckets_t = mine(buckets).T
    rank = mine(factor_order)
    length = lax.dynamic_slice_in_dim(lengths, me, 1, 0)
    bias = masked_bias(length, buckets_t, rank, table)

    q_t = (ein("yde,nd->yen", w_q, stacked).reshape(width, 2 * seq) + q_bias).astype(BF)
    k_t = ein("yde,nd->yen", w_k, content).reshape(width, seq).astype(BF)
    v_t = (ein("yde,nd->yen", w_v, content).reshape(width, seq) + v_bias).astype(BF)
    probs, ctx_t, inverse = attention(q_t, k_t, v_t, bias, heads)
    ctx_parts = ctx_t.reshape(halves, part, 2 * seq)

    resid_one = stacked.astype(F32) + ein("yen,yoe->no", ctx_parts, full_out) + out_bias[0]
    unit_one, inv_one = normalise(resid_one)
    normed = unit_one * gains[0] + shifts[0]
    normed_low = normed.astype(BF)
    hidden = ein("nd,ydf->ynf", normed_low, full_in) + hidden_bias
    cdf = 0.5 * (1.0 + lax.erf(hidden * 0.7071067811865476))
    active = (hidden * cdf).astype(BF)
    slope = (cdf + hidden * (jnp.exp(hidden * hidden * -0.5) * 0.3989422804014327)).astype(BF)
    resid_two = normed + ein("ynf,yof->no", active, full_down) + out_bias[1]
    unit_two, inv_two = normalise(resid_two)
    output = (unit_two * gains[1] + shifts[1]).astype(BF)
    outs = lax.all_gather(output, "y", axis=0).reshape(halves, 2, seq, width)

    cot = jnp.concatenate([mine(cot_content), mine(cot_query)], axis=0).astype(F32)
    d_two = normalise_back(cot * gains[1], unit_two, inv_two)
    d_two_low = d_two.astype(BF)
    d_active = ein("no,yof->ynf", d_two_low, full_down)
    d_hidden = d_active * slope.astype(F32)
    d_hidden_low = d_hidden.astype(BF)
    down_grad = ein("no,ynf->yof", d_two_low, active).astype(BF)
    in_grad = ein("nd,ynf->ydf", normed_low, d_hidden_low).astype(BF)
    d_normed = d_two + ein("ynf,ydf->nd", d_hidden_low, full_in)
    d_one = normalise_back(d_normed * gains[0], unit_one, inv_one)
    d_one_low = d_one.astype(BF)
    out_grad = ein("no,yen->yoe", d_one_low, ctx_parts).astype(BF)
    dctx_t = ein("yoe,no->yen", full_out, d_one_low).reshape(width, 2 * seq).astype(BF)

    blocks = (halves, lax.axis_size("z"), lax.axis_size("x"), 2, rows)
    down_share = scatter_rows(down_grad.reshape(blocks + (ffn,)), ("core", "x", "y", "z"))
    in_out = jnp.concatenate([in_grad, out_grad], axis=-1)
    in_out_share = scatter_rows(in_out.reshape(blocks + (ffn + part,)), ("core", "y", "x", "z"))

    early = jnp.concatenate(
        [
            jnp.sum(d_hidden, axis=1).reshape(-1),
            jnp.sum(d_one, axis=0),
            jnp.sum(d_two, axis=0),
            jnp.sum(d_normed * unit_one, axis=0),
            jnp.sum(cot * unit_two, axis=0),
            jnp.sum(d_normed, axis=0),
            jnp.sum(cot, axis=0),
        ]
    )
    early = sum_all(early.reshape(-1, 128)).reshape(-1)

    dq_t, dk_t, dv_t, table_grad = attention_back(
        q_t, k_t, v_t, probs, inverse, ctx_t, dctx_t, buckets_t, heads, bucket_count
    )
    dq_parts = dq_t.reshape(halves, part, 2 * seq)
    dk_parts = dk_t.reshape(halves, part, seq)
    dv_parts = dv_t.reshape(halves, part, seq)
    qkv_grad = jnp.concatenate(
        [
            ein("nd,yen->yde", stacked, dq_parts),
            ein("nd,yen->yde", content, dk_parts),
            ein("nd,yen->yde", content, dv_parts),
        ],
        axis=-1,
    ).astype(BF)
    qkv_grad = qkv_grad.reshape(blocks + (3 * part,))
    first_share = scatter_rows(qkv_grad[..., :cut], ("core", "x", "y", "z"))
    second_share = scatter_rows(qkv_grad[..., cut:], ("core", "y", "x", "z"))
    qkv_share = jnp.concatenate([first_share, second_share], axis=-1)

    grad_in = ein("yen,yde->nd", dq_parts, w_q)
    extra = ein("yen,yde->nd", dk_parts, w_k) + ein("yen,yde->nd", dv_parts, w_v)
    grad_in = d_one + grad_in
    grad_in = jnp.concatenate([grad_in[:seq] + extra, grad_in[seq:]], axis=0).astype(BF)
    grad_ins = lax.all_to_all(
        grad_in.reshape(1, 2, seq, width), "y", split_axis=3, concat_axis=0, tiled=True
    )

    table_grad = jnp.sum(table_grad.reshape(bucket_count, heads, 16), axis=2).T
    late = jnp.concatenate(
        [
            jnp.sum(dq_t.astype(F32), axis=1),
            jnp.sum(dv_t.astype(F32), axis=1),
            table_grad.reshape(-1),
        ]
    )
    late = sum_all(late.reshape(-1, 128)).reshape(-1)

    grad_b_qv = mine(jnp.transpose(late[: 2 * width].reshape(2, halves, part), (1, 0, 2)))
    grad_table = mine(late[2 * width :].reshape(halves, heads_here, bucket_count)).T
    grad_b_in = mine(early[: halves * ffn].reshape(halves, ffn))
    pairs = early[halves * ffn :].reshape(3, 2, width)
    return (
        outs[:, 0],
        outs[:, 1],
        grad_ins[:, 0],
        grad_ins[:, 1],
        jnp.transpose(qkv_share.reshape(rows, 3, part), (1, 0, 2)),
        grad_b_qv,
        in_out_share[:, ffn:].T,
        in_out_share[:, :ffn],
        grad_b_in,
        down_share.T,
        pairs[0],
        pairs[1],
        pairs[2],
        grad_table,
    )


def solution(mesh):
    count = mesh.shape["dp"] // 2
    depth = 4 if count % 4 == 0 else 1
    while count // depth > depth:
        depth *= 2
    grid = mesh.devices.reshape(depth, count // depth, 2, mesh.shape["tensor"])
    fine = Mesh(grid, ("z", "x", "core", "y"))
    dp = ("z", "x", "core")
    return jax.shard_map(
        shards,
        mesh=fine,
        in_specs=(
            P(dp, None, None),
            P(dp, None, None),
            P(dp),
            P(dp, None),
            P(dp, None, None),
            P(None, dp, "y"),
            P(None, "y"),
            P("y", dp),
            P(dp, "y"),
            P("y"),
            P("y", dp),
            P(),
            P(),
            P(),
            P(None, "y"),
            P(dp, None, None),
            P(dp, None, None),
        ),
        out_specs=(
            P(dp, None, None),
            P(dp, None, None),
            P(dp, None, "y"),
            P(dp, None, "y"),
            P(None, dp, "y"),
            P(None, "y"),
            P("y", dp),
            P(dp, "y"),
            P("y"),
            P("y", dp),
            P(),
            P(),
            P(),
            P(None, "y"),
        ),
        check_vma=False,
    )
```

time: 1110 us -> 467 us (0.42)
  waiting for transfers between devices: 592 us -> 106 us
  matrix products: 212 us -> 101 us
  blocking collectives: 87.9 us -> 0 us
  Pallas kernels: 0 us -> 64.1 us
  starting transfers between devices: 2.44 us -> 60.2 us
  other arithmetic: 97.4 us -> 47.1 us
  local copies, waits for them, and re-layouts: 91.7 us -> 67.8 us
    reduce_scatter x9 -> x0, waiting for transfers between devices: 355 us -> none  [the longest x1 79.6 us: shards(): lax.psum_scatter(step_grads[2], 'dp', scatter_dimension=0, tiled=True)]
    all_gather x9 -> x2, waiting for transfers between devices: 231 us -> 0.01 us  [the longest x1 0.01 us: shards(): lax.all_gather(rest_shard, ('y', 'z', 'x', 'core'), axis=0)]
    dot_general x58 -> x18, matrix products: 212 us -> 101 us  [ein(): return jnp.einsum(spec, a, b, preferred_element_type=F32)]
    ppermute x0 -> x49, waiting for transfers between devices: none -> 106 us  [shifted(): lax.ppermute(value, axis, [(i, (i + step) % size) for i in range(size)])]
    pallas_call x0 -> x3, Pallas kernels: none -> 64.1 us  [the longest x1 30.9 us: attention_back(): pl.pallas_call(functools.partial(backward_kernel, tile=tile, buckets=buck...]
    psum x1 -> x0, blocking collectives: 61.6 us -> none  [shards(): small_totals = lax.psum(small_sums, 'dp')]
    ppermute x0 -> x49, starting transfers between devices: none -> 55.4 us  [shifted(): lax.ppermute(value, axis, [(i, (i + step) % size) for i in range(size)])]
    reduce_sum x20 -> x8, other arithmetic: 54.9 us -> 8.64 us  [the longest x1 3.28 us: shards(): jnp.sum(d_two, axis=0)]
  transfers between devices with their start and end apart: 21 -> 52, of which waited for: 18 -> 21; matrix products, arithmetic and copies ran while one was open for 17% -> 23% of each run, Pallas kernels for 0% -> 7%
where the time goes in v1:
time: 467 us; the launch traced here: 462 us
  waiting for transfers between devices  106 us (23%)
  matrix products  101 us (22%)
  local copies, waits for them, and re-layouts  67.8 us (15%)
  Pallas kernels  64.1 us (14%)
  starting transfers between devices  60.2 us (13%)
  other arithmetic  47.1 us (10%)
  between operations  15.4 us (3%)
    ppermute x49, waiting for transfers between devices, shifted(): lax.ppermute(value, axis, [(i, (i + step) % size) for i in range(size)])  106 us
    dot_general x18, matrix products, ein(): return jnp.einsum(spec, a, b, preferred_element_type=F32)  101 us
    ppermute x49, starting transfers between devices, shifted(): lax.ppermute(value, axis, [(i, (i + step) % size) for i in range(size)])  55.4 us
    pallas_call x1, Pallas kernels, attention_back(): pl.pallas_call(functools.partial(backward_kernel, tile=tile, buckets=buck...  30.9 us
    pallas_call x1, Pallas kernels, attention(): pl.pallas_call(functools.partial(forward_kernel, tile=tile), grid=(heads,...  24.3 us
    convert_element_type x12, other arithmetic, scatter_axis(): return total.astype(BF) if low else total  17 us
    unnamed x106, local copies, waits for them, and re-layouts  13 us
  transfers between devices with their start and end apart: 52, of which 21 were waited for; matrix products, arithmetic and copies ran while one was open for 23% of the time, Pallas kernels for 7%

profile of v1, /device:TPU:0, one launch (start us, length us, event | category | flops | bytes accessed | tf_op | source)
XLA Modules:
  0.0 461.7 jit_solution(17390793226315802553)
XLA Ops:
  10.1 5.1 %collective-permute-start.6 = (bf16[48,512]{1,0:T(8,128)(2,1)S(1)}, bf16[48,512]{1,0:T(8,128)(2,1)S(1)}, u32[]{:S(2)}, u32[]{:S(2)}) collective-permute-start(bf16[48,512]{1,0:T(8,128)(2,1)S(1)} %slice.153), channel_id=1, source_target_pairs={{0,24},{8,0},{16,8},{24,16},{1,25},{9,1},{17,9},{25,17},{2,26},{10... | collective-permute-start | bytes 147464 | tf_op jit(solution)/shard_map/ppermute | solution.py:202
  16.2 2.8 collective-permute-start
  24.1 2.9 dynamic-slice_bitcast_fusion.5
  29.6 4.6 collective-permute-done.2
  36.6 6.7 %collective-permute-done.3 = bf16[4,48,640]{2,1,0:T(8,128)(2,1)S(1)} collective-permute-done((bf16[4,48,640]{2,1,0:T(8,128)(2,1)S(1)}, bf16[4,48,640]{2,1,0:T(8,128)(2,1)S(1)}, u32[]{:S(2)}, u32[]{:S(2)}) %collective-permute-start.3) | collective-permute-done | bytes 245792 | tf_op jit(solution)/shard_map/ppermute | solution.py:202
  45.1 11.0 %collective-permute-done.10 = bf16[2,4,48,512]{3,2,1,0:T(8,128)(2,1)S(1)} collective-permute-done((bf16[2,4,48,512]{3,2,1,0:T(8,128)(2,1)S(1)}, bf16[2,4,48,512]{3,2,1,0:T(8,128)(2,1)S(1)}, u32[]{:S(2)}, u32[]{:S(2)}) %collective-permute-start.10) | collective-permute-done | bytes 393248 | tf_op jit(solution)/shard_map/ppermute | solution.py:202
  59.4 2.5 copy.138
  64.3 8.9 %shard_map.272.bias_ref = bf16[12,512,1024]{2,1,0:T(8,128)(2,1)} custom-call(s32[1]{0:T(128)} %dynamic_slice.172.len_ref, s32[512,512]{1,0:T(8,128)} %bitcast.374, s32[1,512]{1,0:T(1,128)} %constant_dynamic-slice_fusion.5.rank_row_ref, s32[512,1]{1,0:T(8,128)} %copy.140.rank_col_ref, f32[12,128]{1,0:T(8,128)} %pad.9.table_ref), custom_call_target="tpu_custom_call" | custom-call | tf_op jit(solution)/shard_map/pallas_call | solution.py:57
  83.6 3.3 convolution_convert_fusion.4.k_ref
  86.9 2.9 add_convert_fusion.1.v_ref
  89.8 2.7 fusion.49
  93.9 24.3 %shard_map.273 = (bf16[12,512,1024]{2,1,0:T(8,128)(2,1)}, bf16[768,1024]{1,0:T(8,128)(2,1)}, f32[12,1,1024]{2,1,0:T(1,128)}) custom-call(bf16[768,1024]{1,0:T(8,128)(2,1)} %fusion.30.q_ref, bf16[768,512]{1,0:T(8,128)(2,1)} %convolution_convert_fusion.4.k_ref, bf16[768,512]{1,0:T(8,128)(2,1)} %add_convert_fusion.1.v_ref, ...), custom_call_target="tpu_custom_call" | custom-call | tf_op jit(solution)/shard_map/pallas_call | solution.py:91
  118.3 3.7 fusion.119
  124.4 9.4 %fusion.3 = (bf16[2,1024,1536]{2,1,0:T(8,128)(2,1)S(1)}, f32[2,1536,1024]{1,2,0:T(8,128)}) fusion(f32[2,1536]{1,0:T(2,128)S(1)} %bitcast.405, bf16[2,768,3456]{2,1,0:T(8,128)(2,1)S(1)} %bitcast.413, f32[1024,768]{1,0:T(8,128)S(1)} %get-tuple-element.141, f32[768]{0:T(1024)S(1)} %get-tuple-element.81, f32[768]{0:T(1024)S(1)} %get-tuple-element.152, ...), kind=kOutput, calls=%fused_computation.8 | convolution fusion | flops 4854644736 | bytes 26767360 | tf_op jit(solution)/shard_map/nd,ydf->ynf/dot_general | solution.py:268
  133.7 5.4 %fusion.120 = (f32[1024]{0:T(1024)S(1)}, f32[1024,768]{1,0:T(8,128)S(1)}) fusion(f32[768]{0:T(1024)S(1)} %get-tuple-element.82, bf16[2,1024,1536]{2,1,0:T(8,128)(2,1)S(1)} %get-tuple-element.142, bf16[2,768,3456]{2,1,0:T(8,128)(2,1)S(1)} %bitcast.414, f32[768]{0:T(1024)S(1)} %get-tuple-element.81, f32[768]{0:T(1024)S(1)} %get-tuple-element.152, ...), kind=kOutput, calls=%fused_computation.271 | convolution fusion | flops 4837342208 | bytes 17326080 | tf_op jit(solution)/shard_map/ynf,yof->no/dot_general | solution.py:268
  139.7 2.6 fusion.27
  142.4 3.3 fusion.114
  145.7 6.9 %convolution_convert_fusion = bf16[2,1536,768]{1,2,0:T(8,128)(2,1)} fusion(bf16[2,1024,1536]{2,1,0:T(8,128)(2,1)S(1)} %get-tuple-element.142, f32[1024,768]{1,0:T(8,128)S(1)} %get-tuple-element.85), kind=kOutput, calls=%fused_computation.25 | convolution fusion | flops 4834983936 | bytes 14155776 | tf_op jit(solution)/shard_map/no,ynf->yof/dot_general | solution.py:268
  152.6 17.1 %fusion.9 = (f32[2,1536]{1,0:T(2,128)S(1)}, bf16[2,1024,1536]{2,1,0:T(8,128)(2,1)}, f32[2,1536,1024]{1,2,0:T(8,128)}) fusion(f32[2,1536,1024]{1,2,0:T(8,128)} %get-tuple-element.143, f32[2,1536]{1,0:T(2,128)S(1)} %bitcast.406, bf16[2,768,3456]{2,1,0:T(8,128)(2,1)S(1)} %bitcast.415, f32[1024,768]{1,0:T(8,128)S(1)} %get-tuple-element.85), kind=kOutput, calls=%fused_computation.14 | convolution fusion | flops 4873516032 | bytes 39346176 | tf_op jit(solution)/shard_map/no,yof->ynf/dot_general | solution.py:268
  169.7 16.8 %multiply_reduce_fusion = (f32[768]{0:T(1024)S(1)}, f32[1024]{0:T(1024)S(1)}, f32[1024]{0:T(1024)S(1)}, f32[768]{0:T(1024)S(1)}, f32[1024,768]{1,0:T(8,128)}) fusion(f32[1024,768]{1,0:T(8,128)} %copy-done.4, f32[1024]{0:T(1024)S(1)} %add_rsqrt_fusion.1, f32[1024]{0:T(1024)S(1)} %broadcast_multiply_fusion.5, f32[768]{0:T(1024)S(1)} %get-tuple-element.152, ...), kind=kOutput, calls=%fused_computation.50 | convolution fusion | flops 4849135616 | bytes 33055744 | tf_op jit(solution)/shard_map/ynf,ydf->nd/dot_general | solution.py:268
  186.5 12.3 %convert_bitcast_fusion = bf16[2,768,1536]{1,2,0:T(8,128)(2,1)} fusion(f32[1024,768]{1,0:T(8,128)} %copy-done.4, f32[768]{0:T(1024)S(1)} %get-tuple-element.81, f32[768]{0:T(1024)S(1)} %get-tuple-element.152, f32[1024]{0:T(1024)S(1)} %add_rsqrt_fusion.1, f32[1024]{0:T(1024)S(1)} %broadcast_multiply_fusion.5, bf16[2,1024,1536]{2,1,0:T(8,128)(2,1)} %get-tuple-element.89, ...), kind=kOutput, calls=%fused_computation.24 | convolution fusion | flops 4847566848 | bytes 26753024 | tf_op jit(solution)/shard_map/nd,ynf->ydf/dot_general | solution.py:268
  201.7 3.9 convolution_convert_fusion.1
  205.7 30.9 %shard_map.274 = (bf16[768,1024]{1,0:T(8,128)(2,1)}, bf16[768,512]{1,0:T(8,128)(2,1)}, bf16[768,512]{1,0:T(8,128)(2,1)}, f32[32,192]{1,0:T(8,128)}) custom-call(bf16[768,1024]{1,0:T(8,128)(2,1)} %fusion.30.q_ref, bf16[768,512]{1,0:T(8,128)(2,1)} %convolution_convert_fusion.4.k_ref, bf16[768,512]{1,0:T(8,128)(2,1)} %add_convert_fusion.1.v_ref, ...), custom_call_target="tpu_custom_call" | custom-call | tf_op jit(solution)/shard_map/pallas_call | solution.py:172
  236.6 3.3 fusion.58
  242.2 2.4 fusion.63
  244.6 3.1 bitcast_add_fusion
  251.5 5.2 %pad_maximum_fusion = bf16[2,768,1920]{1,2,0:T(8,128)(2,1)} fusion(bf16[2,768,384]{1,2,0:T(8,128)(2,1)S(1)} %fusion.60, bf16[2,768,1536]{1,2,0:T(8,128)(2,1)} %convert_bitcast_fusion), kind=kLoop, calls=%fused_computation.16 | loop fusion | flops 11796480 | bytes 11796480 | tf_op jit(solution)/shard_map/concatenate | solution.py:375
  256.7 8.6 %copy.158 = bf16[2,768,1920]{2,1,0:T(8,128)(2,1)} copy(bf16[2,768,1920]{1,2,0:T(8,128)(2,1)} %pad_maximum_fusion) | data formatting | bytes 11796480 | tf_op jit(solution)/shard_map/concatenate | solution.py:375
  265.2 3.8 dynamic-slice_bitcast_fusion
  278.4 2.5 fusion.80
  282.0 3.0 collective-permute-start.26
  289.9 4.9 %copy.149 = bf16[1,2,512,768]{2,1,0,3:T(2,128)(2,1)} copy(bf16[1,2,512,768]{3,2,1,0:T(8,128)(2,1)} %bitcast.377) | data formatting | bytes 3145728 | tf_op jit(solution)/shard_map/convert_element_type | solution.py:413
  294.8 4.7 %all-to-all-start = ((bf16[1,2,512,768]{2,1,0,3:T(2,128)(2,1)}), bf16[1,2,512,768]{2,1,0,3:T(2,128)(2,1)}, u32[]{:S(2)}, u32[]{:S(2)}) async-start(bf16[1,2,512,768]{2,1,0,3:T(2,128)(2,1)} %copy.149), calls=%async_computation | async-start | bytes 3145728 | tf_op jit(solution)/shard_map/all_to_all | solution.py:414
  300.9 3.3 collective-permute-start.30
  312.4 16.5 %collective-permute-done.39 = f32[60,128]{1,0:T(8,128)S(1)} collective-permute-done((f32[60,128]{1,0:T(8,128)S(1)}, f32[60,128]{1,0:T(8,128)S(1)}, u32[]{:S(2)}, u32[]{:S(2)}) %collective-permute-start.39) | collective-permute-done | bytes 30752 | tf_op jit(solution)/shard_map/ppermute | solution.py:202
  329.0 4.0 collective-permute-start.42
  347.4 13.9 %collective-permute-done.20 = bf16[4,2,48,512]{3,2,0,1:T(8,128)(2,1)} collective-permute-done((bf16[4,2,48,512]{3,2,0,1:T(8,128)(2,1)}, bf16[4,2,48,512]{3,2,0,1:T(8,128)(2,1)}, u32[]{:S(2)}, u32[]{:S(2)}) %collective-permute-start.20) | collective-permute-done | bytes 393248 | tf_op jit(solution)/shard_map/ppermute | solution.py:202
  364.7 3.6 collective-permute-done.21
  372.6 2.5 fusion.12
  376.5 2.5 fusion.11
  383.1 2.8 collective-permute-start.18
  389.3 10.9 %collective-permute-done.44 = bf16[2,4,48,1536]{3,2,1,0:T(8,128)(2,1)} collective-permute-done((bf16[2,4,48,1536]{3,2,1,0:T(8,128)(2,1)S(1)}, bf16[2,4,48,1536]{3,2,1,0:T(8,128)(2,1)}, u32[]{:S(2)}, u32[]{:S(2)}) %collective-permute-start.44) | collective-permute-done | bytes 1179680 | tf_op jit(solution)/shard_map/ppermute | solution.py:202
  403.1 13.0 %collective-permute-done.32 = bf16[4,2,48,1920]{3,2,1,0:T(8,128)(2,1)} collective-permute-done((bf16[4,2,48,1920]{3,2,1,0:T(8,128)(2,1)S(1)}, bf16[4,2,48,1920]{3,2,1,0:T(8,128)(2,1)}, u32[]{:S(2)}, u32[]{:S(2)}) %collective-permute-start.32) | collective-permute-done | bytes 1474592 | tf_op jit(solution)/shard_map/ppermute | solution.py:202
  420.1 3.7 slice_bitcast_fusion
  428.1 2.7 collective-permute-start.48
  434.6 2.6 collective-permute-start.36
  437.2 6.0 %collective-permute-done.47 = bf16[48,1536]{1,0:T(8,128)(2,1)S(1)} collective-permute-done((bf16[48,1536]{1,0:T(8,128)(2,1)S(1)}, bf16[48,1536]{1,0:T(8,128)(2,1)S(1)}, u32[]{:S(2)}, u32[]{:S(2)}) %collective-permute-start.47) | collective-permute-done | bytes 147488 | tf_op jit(solution)/shard_map/ppermute | solution.py:202
  444.4 8.6 %collective-permute-done.35 = bf16[48,1920]{1,0:T(8,128)(2,1)S(1)} collective-permute-done((bf16[48,1920]{1,0:T(8,128)(2,1)S(1)}, bf16[48,1920]{1,0:T(8,128)(2,1)S(1)}, u32[]{:S(2)}, u32[]{:S(2)}) %collective-permute-start.35) | collective-permute-done | bytes 184352 | tf_op jit(solution)/shard_map/ppermute | solution.py:202
  (327 shorter events, 117.8 us)
Async XLA Ops:
  7.2 111.0 %all-gather.5.cloned.1.call-start = ((), (), s32[]{:S(2)}) async-start(), calls=%async_computation.1 | async-start | bytes 10948608 | tf_op jit(solution)/shard_map/all_gather | solution.py:311
  10.1 17.1 %collective-permute-start.6 = (bf16[48,512]{1,0:T(8,128)(2,1)S(1)}, bf16[48,512]{1,0:T(8,128)(2,1)S(1)}, u32[]{:S(2)}, u32[]{:S(2)}) collective-permute-start(bf16[48,512]{1,0:T(8,128)(2,1)S(1)} %slice.153), channel_id=1, source_target_pairs={{0,24},{8,0},{16,8},{24,16},{1,25},{9,1},{17,9},{25,17},{2,26},{10... | collective-permute-start | bytes 147464 | tf_op jit(solution)/shard_map/ppermute | solution.py:202
  15.2 12.3 %collective-permute-start.7 = (bf16[48,512]{1,0:T(8,128)(2,1)S(1)}, bf16[48,512]{1,0:T(8,128)(2,1)S(1)}, u32[]{:S(2)}, u32[]{:S(2)}) collective-permute-start(bf16[48,512]{1,0:T(8,128)(2,1)S(1)} %slice.153), channel_id=1, source_target_pairs={{0,16},{8,24},{16,0},{24,8},{1,17},{9,25},{17,1},{25,9},{2,18},{10... | collective-permute-start | bytes 147464 | tf_op jit(solution)/shard_map/ppermute | solution.py:202
  15.2 13.8 %collective-permute-start.8 = (bf16[48,512]{1,0:T(8,128)(2,1)S(1)}, bf16[48,512]{1,0:T(8,128)(2,1)S(1)}, u32[]{:S(2)}, u32[]{:S(2)}) collective-permute-start(bf16[48,512]{1,0:T(8,128)(2,1)S(1)} %slice.153), channel_id=1, source_target_pairs={{0,8},{8,16},{16,24},{24,0},{1,9},{9,17},{17,25},{25,1},{2,10},{10... | collective-permute-start | bytes 147464 | tf_op jit(solution)/shard_map/ppermute | solution.py:202
  16.2 13.4 %collective-permute-start = (bf16[48,640]{1,0:T(8,128)(2,1)S(1)}, bf16[48,640]{1,0:T(8,128)(2,1)S(1)}, u32[]{:S(2)}, u32[]{:S(2)}) collective-permute-start(bf16[48,640]{1,0:T(8,128)(2,1)S(1)} %slice.152), channel_id=1, source_target_pairs={{0,24},{8,0},{16,8},{24,16},{1,25},{9,1},{17,9},{25,17},{2,26},{10... | collective-permute-start | bytes 184328 | tf_op jit(solution)/shard_map/ppermute | solution.py:202
  19.0 10.6 %collective-permute-start.1 = (bf16[48,640]{1,0:T(8,128)(2,1)S(1)}, bf16[48,640]{1,0:T(8,128)(2,1)S(1)}, u32[]{:S(2)}, u32[]{:S(2)}) collective-permute-start(bf16[48,640]{1,0:T(8,128)(2,1)S(1)} %slice.152), channel_id=1, source_target_pairs={{0,16},{8,24},{16,0},{24,8},{1,17},{9,25},{17,1},{25,9},{2,18},{10... | collective-permute-start | bytes 184328 | tf_op jit(solution)/shard_map/ppermute | solution.py:202
  27.2 7.0 %collective-permute-start.2 = (bf16[48,640]{1,0:T(8,128)(2,1)S(1)}, bf16[48,640]{1,0:T(8,128)(2,1)S(1)}, u32[]{:S(2)}, u32[]{:S(2)}) collective-permute-start(bf16[48,640]{1,0:T(8,128)(2,1)S(1)} %slice.152), channel_id=1, source_target_pairs={{0,8},{8,16},{16,24},{24,0},{1,9},{9,17},{17,25},{25,1},{2,10},{10... | collective-permute-start | bytes 184328 | tf_op jit(solution)/shard_map/ppermute | solution.py:202
  27.5 35.9 %collective-permute-start.12 = (bf16[38,384]{1,0:T(8,128)(2,1)S(1)}, bf16[38,384]{1,0:T(8,128)(2,1)S(1)}, u32[]{:S(2)}, u32[]{:S(2)}) collective-permute-start(bf16[38,384]{1,0:T(8,128)(2,1)S(1)} %fusion.102), channel_id=1, source_target_pairs={{0,1},{1,0},{2,3},{3,2},{4,5},{5,4},{6,7},{7,6},{8,9},{9,8},{10,11... | collective-permute-start | bytes 87560 | tf_op jit(solution)/shard_map/ppermute | solution.py:202
  29.1 6.9 %collective-permute-start.9 = (bf16[4,48,512]{2,1,0:T(8,128)(2,1)S(1)}, bf16[4,48,512]{2,1,0:T(8,128)(2,1)S(1)}, u32[]{:S(2)}, u32[]{:S(2)}) collective-permute-start(bf16[4,48,512]{2,1,0:T(8,128)(2,1)S(1)} %pad_maximum_fusion.15), channel_id=1, source_target_pairs={{0,1},{1,0},{2,3},{3,2},{4,5},{5,4},{6,7},{7,6},{8,9},{9,8},{10,11... | collective-permute-start | bytes 589832 | tf_op jit(solution)/shard_map/ppermute | solution.py:202
  34.3 9.0 %collective-permute-start.3 = (bf16[4,48,640]{2,1,0:T(8,128)(2,1)S(1)}, bf16[4,48,640]{2,1,0:T(8,128)(2,1)S(1)}, u32[]{:S(2)}, u32[]{:S(2)}) collective-permute-start(bf16[4,48,640]{2,1,0:T(8,128)(2,1)S(1)} %pad_maximum_fusion.13), channel_id=1, source_target_pairs={{0,4},{4,0},{1,5},{5,1},{2,6},{6,2},{3,7},{7,3},{8,12},{12,8},{9,1... | collective-permute-start | bytes 737288 | tf_op jit(solution)/shard_map/ppermute | solution.py:202
  36.0 20.0 %collective-permute-start.10 = (bf16[2,4,48,512]{3,2,1,0:T(8,128)(2,1)S(1)}, bf16[2,4,48,512]{3,2,1,0:T(8,128)(2,1)S(1)}, u32[]{:S(2)}, u32[]{:S(2)}) collective-permute-start(bf16[2,4,48,512]{3,2,1,0:T(8,128)(2,1)S(1)} %pad_maximum_fusion.11), channel_id=1, source_target_pairs={{0,4},{4,0},{1,5},{5,1},{2,6},{6,2},{3,7},{7,3},{8,12},{12,8},{9,1... | collective-permute-start | bytes 1179656 | tf_op jit(solution)/shard_map/ppermute | solution.py:202
  43.4 13.7 %collective-permute-start.4 = (bf16[4,2,48,640]{3,2,0,1:T(8,128)(2,1)S(1)}, bf16[4,2,48,640]{3,2,0,1:T(8,128)(2,1)S(1)}, u32[]{:S(2)}, u32[]{:S(2)}) collective-permute-start(bf16[4,2,48,640]{3,2,0,1:T(8,128)(2,1)S(1)} %pad_maximum_fusion.8), channel_id=1, source_target_pairs={{0,1},{1,0},{2,3},{3,2},{4,5},{5,4},{6,7},{7,6},{8,9},{9,8},{10,11... | collective-permute-start | bytes 1474568 | tf_op jit(solution)/shard_map/ppermute | solution.py:202
  57.1 16.1 %collective-permute-start.11 = (bf16[2,4,2,48,512]{4,3,1,0,2:T(8,128)(2,1)}, bf16[2,4,2,48,512]{4,3,1,0,2:T(8,128)(2,1)}, u32[]{:S(2)}, u32[]{:S(2)}) collective-permute-start(bf16[2,4,2,48,512]{4,3,1,0,2:T(8,128)(2,1)} %pad_maximum_fusion.7), channel_id=1, source_target_pairs={{0,2},{2,0},{1,3},{3,1},{4,6},{6,4},{5,7},{7,5},{8,10},{10,8},{9,1... | collective-permute-start | bytes 2359304 | tf_op jit(solution)/shard_map/ppermute | solution.py:202
  58.3 16.2 %collective-permute-start.5 = (bf16[2,4,2,48,640]{4,3,1,2,0:T(8,128)(2,1)}, bf16[2,4,2,48,640]{4,3,1,2,0:T(8,128)(2,1)}, u32[]{:S(2)}, u32[]{:S(2)}) collective-permute-start(bf16[2,4,2,48,640]{4,3,1,2,0:T(8,128)(2,1)} %pad_maximum_fusion.6), channel_id=1, source_target_pairs={{0,2},{2,0},{1,3},{3,1},{4,6},{6,4},{5,7},{7,5},{8,10},{10,8},{9,1... | collective-permute-start | bytes 2949128 | tf_op jit(solution)/shard_map/ppermute | solution.py:202
  251.4 49.6 %collective-permute-start.37 = (f32[60,128]{1,0:T(8,128)S(1)}, f32[60,128]{1,0:T(8,128)S(1)}, u32[]{:S(2)}, u32[]{:S(2)}) collective-permute-start(f32[60,128]{1,0:T(8,128)S(1)} %bitcast.399), channel_id=1, source_target_pairs={{0,2},{2,0},{1,3},{3,1},{4,6},{6,4},{5,7},{7,5},{8,10},{10,8},{9,1... | collective-permute-start | bytes 92168 | tf_op jit(solution)/shard_map/ppermute | solution.py:202
  269.5 12.5 %collective-permute-start.25 = (f32[15,128]{1,0:T(8,128)S(1)}, f32[15,128]{1,0:T(8,128)S(1)}, u32[]{:S(2)}, u32[]{:S(2)}) collective-permute-start(f32[15,128]{1,0:T(8,128)S(1)} %maximum_bitcast_fusion), channel_id=1, source_target_pairs={{0,2},{2,0},{1,3},{3,1},{4,6},{6,4},{5,7},{7,5},{8,10},{10,8},{9,1... | collective-permute-start | bytes 23048 | tf_op jit(solution)/shard_map/ppermute | solution.py:202
  273.5 69.1 %collective-permute-start.13 = (bf16[2,4,2,48,640]{4,3,2,1,0:T(8,128)(2,1)}, bf16[2,4,2,48,640]{4,3,2,1,0:T(8,128)(2,1)}, u32[]{:S(2)}, u32[]{:S(2)}) collective-permute-start(bf16[2,4,2,48,640]{4,3,2,1,0:T(8,128)(2,1)} %fusion.75), channel_id=1, source_target_pairs={{0,2},{2,0},{1,3},{3,1},{4,6},{6,4},{5,7},{7,5},{8,10},{10,8},{9,1... | collective-permute-start | bytes 2949128 | tf_op jit(solution)/shard_map/ppermute | solution.py:202
  281.8 56.1 %collective-permute-start.19 = (bf16[2,4,2,48,512]{4,3,1,2,0:T(8,128)(2,1)}, bf16[2,4,2,48,512]{4,3,1,2,0:T(8,128)(2,1)}, u32[]{:S(2)}, u32[]{:S(2)}) collective-permute-start(bf16[2,4,2,48,512]{4,3,1,2,0:T(8,128)(2,1)} %bitcast.357), channel_id=1, source_target_pairs={{0,2},{2,0},{1,3},{3,1},{4,6},{6,4},{5,7},{7,5},{8,10},{10,8},{9,1... | collective-permute-start | bytes 2359304 | tf_op jit(solution)/shard_map/ppermute | solution.py:202
  287.1 13.2 %collective-permute-start.27 = (f32[15,128]{1,0:T(8,128)S(1)}, f32[15,128]{1,0:T(8,128)S(1)}, u32[]{:S(2)}, u32[]{:S(2)}) collective-permute-start(f32[15,128]{1,0:T(8,128)S(1)} %fusion.138), channel_id=1, source_target_pairs={{0,1},{1,0},{2,3},{3,2},{4,5},{5,4},{6,7},{7,6},{8,9},{9,8},{10,11... | collective-permute-start | bytes 23048 | tf_op jit(solution)/shard_map/ppermute | solution.py:202
  294.8 46.2 %all-to-all-start = ((bf16[1,2,512,768]{2,1,0,3:T(2,128)(2,1)}), bf16[1,2,512,768]{2,1,0,3:T(2,128)(2,1)}, u32[]{:S(2)}, u32[]{:S(2)}) async-start(bf16[1,2,512,768]{2,1,0,3:T(2,128)(2,1)} %copy.149), calls=%async_computation | async-start | bytes 3145728 | tf_op jit(solution)/shard_map/all_to_all | solution.py:414
  299.6 120.5 %all-gather.7.cloned.1.call-start = ((), (), s32[]{:S(2)}) async-start(), calls=%async_computation.2 | async-start | bytes 4718592 | tf_op jit(solution)/shard_map/all_gather | solution.py:357
  300.4 6.9 %collective-permute-start.29 = (f32[15,128]{1,0:T(8,128)S(1)}, f32[15,128]{1,0:T(8,128)S(1)}, u32[]{:S(2)}, u32[]{:S(2)}) collective-permute-start(f32[15,128]{1,0:T(8,128)S(1)} %add.459), channel_id=1, source_target_pairs={{0,16},{8,24},{16,0},{24,8},{1,17},{9,25},{17,1},{25,9},{2,18},{10... | collective-permute-start | bytes 23048 | tf_op jit(solution)/shard_map/ppermute | solution.py:202
  300.9 6.4 %collective-permute-start.30 = (f32[15,128]{1,0:T(8,128)S(1)}, f32[15,128]{1,0:T(8,128)S(1)}, u32[]{:S(2)}, u32[]{:S(2)}) collective-permute-start(f32[15,128]{1,0:T(8,128)S(1)} %add.459), channel_id=1, source_target_pairs={{0,24},{8,0},{16,8},{24,16},{1,25},{9,1},{17,9},{25,17},{2,26},{10... | collective-permute-start | bytes 23048 | tf_op jit(solution)/shard_map/ppermute | solution.py:202
  309.8 19.1 %collective-permute-start.39 = (f32[60,128]{1,0:T(8,128)S(1)}, f32[60,128]{1,0:T(8,128)S(1)}, u32[]{:S(2)}, u32[]{:S(2)}) collective-permute-start(f32[60,128]{1,0:T(8,128)S(1)} %fusion.135), channel_id=1, source_target_pairs={{0,1},{1,0},{2,3},{3,2},{4,5},{5,4},{6,7},{7,6},{8,9},{9,8},{10,11... | collective-permute-start | bytes 92168 | tf_op jit(solution)/shard_map/ppermute | solution.py:202
  328.9 5.7 %collective-permute-start.40 = (f32[60,128]{1,0:T(8,128)S(1)}, f32[60,128]{1,0:T(8,128)S(1)}, u32[]{:S(2)}, u32[]{:S(2)}) collective-permute-start(f32[60,128]{1,0:T(8,128)S(1)} %add.471), channel_id=1, source_target_pairs={{0,8},{8,16},{16,24},{24,0},{1,9},{9,17},{17,25},{25,1},{2,10},{10... | collective-permute-start | bytes 92168 | tf_op jit(solution)/shard_map/ppermute | solution.py:202
  328.9 5.7 %collective-permute-start.41 = (f32[60,128]{1,0:T(8,128)S(1)}, f32[60,128]{1,0:T(8,128)S(1)}, u32[]{:S(2)}, u32[]{:S(2)}) collective-permute-start(f32[60,128]{1,0:T(8,128)S(1)} %add.471), channel_id=1, source_target_pairs={{0,16},{8,24},{16,0},{24,8},{1,17},{9,25},{17,1},{25,9},{2,18},{10... | collective-permute-start | bytes 92168 | tf_op jit(solution)/shard_map/ppermute | solution.py:202
  329.0 6.4 %collective-permute-start.42 = (f32[60,128]{1,0:T(8,128)S(1)}, f32[60,128]{1,0:T(8,128)S(1)}, u32[]{:S(2)}, u32[]{:S(2)}) collective-permute-start(f32[60,128]{1,0:T(8,128)S(1)} %add.471), channel_id=1, source_target_pairs={{0,24},{8,0},{16,8},{24,16},{1,25},{9,1},{17,9},{25,17},{2,26},{10... | collective-permute-start | bytes 92168 | tf_op jit(solution)/shard_map/ppermute | solution.py:202
  334.6 37.9 %collective-permute-start.43 = (bf16[2,4,2,48,1536]{4,3,1,0,2:T(8,128)(2,1)}, bf16[2,4,2,48,1536]{4,3,1,0,2:T(8,128)(2,1)}, u32[]{:S(2)}, u32[]{:S(2)}) collective-permute-start(bf16[2,4,2,48,1536]{4,3,1,0,2:T(8,128)(2,1)} %bitcast.385), channel_id=1, source_target_pairs={{0,2},{2,0},{1,3},{3,1},{4,6},{6,4},{5,7},{7,5},{8,10},{10,8},{9,1... | collective-permute-start | bytes 7077896 | tf_op jit(solution)/shard_map/ppermute | solution.py:202
  334.6 41.8 %collective-permute-start.31 = (bf16[2,4,2,48,1920]{4,3,2,1,0:T(8,128)(2,1)}, bf16[2,4,2,48,1920]{4,3,2,1,0:T(8,128)(2,1)}, u32[]{:S(2)}, u32[]{:S(2)}) collective-permute-start(bf16[2,4,2,48,1920]{4,3,2,1,0:T(8,128)(2,1)} %dynamic-slice_bitcast_fusion), channel_id=1, source_target_pairs={{0,2},{2,0},{1,3},{3,1},{4,6},{6,4},{5,7},{7,5},{8,10},{10,8},{9,1... | collective-permute-start | bytes 8847368 | tf_op jit(solution)/shard_map/ppermute | solution.py:202
  341.0 20.3 %collective-permute-start.20 = (bf16[4,2,48,512]{3,2,0,1:T(8,128)(2,1)}, bf16[4,2,48,512]{3,2,0,1:T(8,128)(2,1)}, u32[]{:S(2)}, u32[]{:S(2)}) collective-permute-start(bf16[4,2,48,512]{3,2,0,1:T(8,128)(2,1)} %dynamic-slice_bitcast_fusion.10), channel_id=1, source_target_pairs={{0,1},{1,0},{2,3},{3,2},{4,5},{5,4},{6,7},{7,6},{8,9},{9,8},{10,11... | collective-permute-start | bytes 1179656 | tf_op jit(solution)/shard_map/ppermute | solution.py:202
  344.2 19.1 %collective-permute-start.14 = (bf16[2,4,48,640]{3,2,1,0:T(8,128)(2,1)S(1)}, bf16[2,4,48,640]{3,2,1,0:T(8,128)(2,1)}, u32[]{:S(2)}, u32[]{:S(2)}) collective-permute-start(bf16[2,4,48,640]{3,2,1,0:T(8,128)(2,1)S(1)} %dynamic-slice_bitcast_fusion.9), channel_id=1, source_target_pairs={{0,4},{4,0},{1,5},{5,1},{2,6},{6,2},{3,7},{7,3},{8,12},{12,8},{9,1... | collective-permute-start | bytes 1474568 | tf_op jit(solution)/shard_map/ppermute | solution.py:202
  362.6 5.7 %collective-permute-start.21 = (bf16[4,48,512]{2,1,0:T(8,128)(2,1)S(1)}, bf16[4,48,512]{2,1,0:T(8,128)(2,1)S(1)}, u32[]{:S(2)}, u32[]{:S(2)}) collective-permute-start(bf16[4,48,512]{2,1,0:T(8,128)(2,1)S(1)} %dynamic-slice_bitcast_fusion.12), channel_id=1, source_target_pairs={{0,4},{4,0},{1,5},{5,1},{2,6},{6,2},{3,7},{7,3},{8,12},{12,8},{9,1... | collective-permute-start | bytes 589832 | tf_op jit(solution)/shard_map/ppermute | solution.py:202
  364.5 6.5 %collective-permute-start.15 = (bf16[4,48,640]{2,1,0:T(8,128)(2,1)S(1)}, bf16[4,48,640]{2,1,0:T(8,128)(2,1)S(1)}, u32[]{:S(2)}, u32[]{:S(2)}) collective-permute-start(bf16[4,48,640]{2,1,0:T(8,128)(2,1)S(1)} %dynamic-slice_bitcast_fusion.11), channel_id=1, source_target_pairs={{0,1},{1,0},{2,3},{3,2},{4,5},{5,4},{6,7},{7,6},{8,9},{9,8},{10,11... | collective-permute-start | bytes 737288 | tf_op jit(solution)/shard_map/ppermute | solution.py:202
  368.4 12.6 %collective-permute-start.22 = (bf16[48,512]{1,0:T(8,128)(2,1)S(1)}, bf16[48,512]{1,0:T(8,128)(2,1)S(1)}, u32[]{:S(2)}, u32[]{:S(2)}) collective-permute-start(bf16[48,512]{1,0:T(8,128)(2,1)S(1)} %get-tuple-element.130), channel_id=1, source_target_pairs={{0,8},{8,16},{16,24},{24,0},{1,9},{9,17},{17,25},{25,1},{2,10},{10... | collective-permute-start | bytes 147464 | tf_op jit(solution)/shard_map/ppermute | solution.py:202
  368.5 13.5 %collective-permute-start.23 = (bf16[48,512]{1,0:T(8,128)(2,1)S(1)}, bf16[48,512]{1,0:T(8,128)(2,1)S(1)}, u32[]{:S(2)}, u32[]{:S(2)}) collective-permute-start(bf16[48,512]{1,0:T(8,128)(2,1)S(1)} %get-tuple-element.132), channel_id=1, source_target_pairs={{0,16},{8,24},{16,0},{24,8},{1,17},{9,25},{17,1},{25,9},{2,18},{10... | collective-permute-start | bytes 147464 | tf_op jit(solution)/shard_map/ppermute | solution.py:202
  371.1 12.1 %collective-permute-start.24 = (bf16[48,512]{1,0:T(8,128)(2,1)S(1)}, bf16[48,512]{1,0:T(8,128)(2,1)S(1)}, u32[]{:S(2)}, u32[]{:S(2)}) collective-permute-start(bf16[48,512]{1,0:T(8,128)(2,1)S(1)} %get-tuple-element.131), channel_id=1, source_target_pairs={{0,24},{8,0},{16,8},{24,16},{1,25},{9,1},{17,9},{25,17},{2,26},{10... | collective-permute-start | bytes 147464 | tf_op jit(solution)/shard_map/ppermute | solution.py:202
  375.2 25.0 %collective-permute-start.44 = (bf16[2,4,48,1536]{3,2,1,0:T(8,128)(2,1)S(1)}, bf16[2,4,48,1536]{3,2,1,0:T(8,128)(2,1)}, u32[]{:S(2)}, u32[]{:S(2)}) collective-permute-start(bf16[2,4,48,1536]{3,2,1,0:T(8,128)(2,1)S(1)} %dynamic-slice_bitcast_fusion.2), channel_id=1, source_target_pairs={{0,4},{4,0},{1,5},{5,1},{2,6},{6,2},{3,7},{7,3},{8,12},{12,8},{9,1... | collective-permute-start | bytes 3538952 | tf_op jit(solution)/shard_map/ppermute | solution.py:202
  380.7 35.4 %collective-permute-start.32 = (bf16[4,2,48,1920]{3,2,1,0:T(8,128)(2,1)S(1)}, bf16[4,2,48,1920]{3,2,1,0:T(8,128)(2,1)}, u32[]{:S(2)}, u32[]{:S(2)}) collective-permute-start(bf16[4,2,48,1920]{3,2,1,0:T(8,128)(2,1)S(1)} %dynamic-slice_bitcast_fusion.1), channel_id=1, source_target_pairs={{0,1},{1,0},{2,3},{3,2},{4,5},{5,4},{6,7},{7,6},{8,9},{9,8},{10,11... | collective-permute-start | bytes 4423688 | tf_op jit(solution)/shard_map/ppermute | solution.py:202
  381.0 6.2 %collective-permute-start.16 = (bf16[48,640]{1,0:T(8,128)(2,1)S(1)}, bf16[48,640]{1,0:T(8,128)(2,1)S(1)}, u32[]{:S(2)}, u32[]{:S(2)}) collective-permute-start(bf16[48,640]{1,0:T(8,128)(2,1)S(1)} %get-tuple-element.127), channel_id=1, source_target_pairs={{0,8},{8,16},{16,24},{24,0},{1,9},{9,17},{17,25},{25,1},{2,10},{10... | collective-permute-start | bytes 184328 | tf_op jit(solution)/shard_map/ppermute | solution.py:202
  381.9 6.4 %collective-permute-start.17 = (bf16[48,640]{1,0:T(8,128)(2,1)S(1)}, bf16[48,640]{1,0:T(8,128)(2,1)S(1)}, u32[]{:S(2)}, u32[]{:S(2)}) collective-permute-start(bf16[48,640]{1,0:T(8,128)(2,1)S(1)} %get-tuple-element.129), channel_id=1, source_target_pairs={{0,16},{8,24},{16,0},{24,8},{1,17},{9,25},{17,1},{25,9},{2,18},{10... | collective-permute-start | bytes 184328 | tf_op jit(solution)/shard_map/ppermute | solution.py:202
  402.2 22.6 %collective-permute-start.45 = (bf16[4,48,1536]{2,1,0:T(8,128)(2,1)S(1)}, bf16[4,48,1536]{2,1,0:T(8,128)(2,1)}, u32[]{:S(2)}, u32[]{:S(2)}) collective-permute-start(bf16[4,48,1536]{2,1,0:T(8,128)(2,1)S(1)} %dynamic-slice_bitcast_fusion.8), channel_id=1, source_target_pairs={{0,1},{1,0},{2,3},{3,2},{4,5},{5,4},{6,7},{7,6},{8,9},{9,8},{10,11... | collective-permute-start | bytes 1769480 | tf_op jit(solution)/shard_map/ppermute | solution.py:202
  419.3 11.8 %collective-permute-start.33 = (bf16[4,48,1920]{2,1,0:T(8,128)(2,1)}, bf16[4,48,1920]{2,1,0:T(8,128)(2,1)}, u32[]{:S(2)}, u32[]{:S(2)}) collective-permute-start(bf16[4,48,1920]{2,1,0:T(8,128)(2,1)} %dynamic-slice_bitcast_fusion.6), channel_id=1, source_target_pairs={{0,4},{4,0},{1,5},{5,1},{2,6},{6,2},{3,7},{7,3},{8,12},{12,8},{9,1... | collective-permute-start | bytes 2211848 | tf_op jit(solution)/shard_map/ppermute | solution.py:202
  426.2 8.4 %collective-permute-start.46 = (bf16[48,1536]{1,0:T(8,128)(2,1)S(1)}, bf16[48,1536]{1,0:T(8,128)(2,1)S(1)}, u32[]{:S(2)}, u32[]{:S(2)}) collective-permute-start(bf16[48,1536]{1,0:T(8,128)(2,1)S(1)} %get-tuple-element.112), channel_id=1, source_target_pairs={{0,8},{8,16},{16,24},{24,0},{1,9},{9,17},{17,25},{25,1},{2,10},{10... | collective-permute-start | bytes 442376 | tf_op jit(solution)/shard_map/ppermute | solution.py:202
  427.3 16.0 %collective-permute-start.47 = (bf16[48,1536]{1,0:T(8,128)(2,1)S(1)}, bf16[48,1536]{1,0:T(8,128)(2,1)S(1)}, u32[]{:S(2)}, u32[]{:S(2)}) collective-permute-start(bf16[48,1536]{1,0:T(8,128)(2,1)S(1)} %get-tuple-element.114), channel_id=1, source_target_pairs={{0,16},{8,24},{16,0},{24,8},{1,17},{9,25},{17,1},{25,9},{2,18},{10... | collective-permute-start | bytes 442376 | tf_op jit(solution)/shard_map/ppermute | solution.py:202
  428.1 15.1 %collective-permute-start.48 = (bf16[48,1536]{1,0:T(8,128)(2,1)S(1)}, bf16[48,1536]{1,0:T(8,128)(2,1)S(1)}, u32[]{:S(2)}, u32[]{:S(2)}) collective-permute-start(bf16[48,1536]{1,0:T(8,128)(2,1)S(1)} %get-tuple-element.113), channel_id=1, source_target_pairs={{0,24},{8,0},{16,8},{24,16},{1,25},{9,1},{17,9},{25,17},{2,26},{10... | collective-permute-start | bytes 442376 | tf_op jit(solution)/shard_map/ppermute | solution.py:202
  432.4 12.0 %collective-permute-start.34 = (bf16[48,1920]{1,0:T(8,128)(2,1)S(1)}, bf16[48,1920]{1,0:T(8,128)(2,1)S(1)}, u32[]{:S(2)}, u32[]{:S(2)}) collective-permute-start(bf16[48,1920]{1,0:T(8,128)(2,1)S(1)} %get-tuple-element.109), channel_id=1, source_target_pairs={{0,8},{8,16},{16,24},{24,0},{1,9},{9,17},{17,25},{25,1},{2,10},{10... | collective-permute-start | bytes 552968 | tf_op jit(solution)/shard_map/ppermute | solution.py:202
  433.2 19.9 %collective-permute-start.35 = (bf16[48,1920]{1,0:T(8,128)(2,1)S(1)}, bf16[48,1920]{1,0:T(8,128)(2,1)S(1)}, u32[]{:S(2)}, u32[]{:S(2)}) collective-permute-start(bf16[48,1920]{1,0:T(8,128)(2,1)S(1)} %get-tuple-element.111), channel_id=1, source_target_pairs={{0,16},{8,24},{16,0},{24,8},{1,17},{9,25},{17,1},{25,9},{2,18},{10... | collective-permute-start | bytes 552968 | tf_op jit(solution)/shard_map/ppermute | solution.py:202
  434.6 18.5 %collective-permute-start.36 = (bf16[48,1920]{1,0:T(8,128)(2,1)S(1)}, bf16[48,1920]{1,0:T(8,128)(2,1)S(1)}, u32[]{:S(2)}, u32[]{:S(2)}) collective-permute-start(bf16[48,1920]{1,0:T(8,128)(2,1)S(1)} %get-tuple-element.110), channel_id=1, source_target_pairs={{0,24},{8,0},{16,8},{24,16},{1,25},{9,1},{17,9},{25,17},{2,26},{10... | collective-permute-start | bytes 552968 | tf_op jit(solution)/shard_map/ppermute | solution.py:202
  (51 other events, 367.4 us)
Sparse Core Ops, SparseCore 0:
  10.9 95.2 all-gather.4
  302.0 60.2 all-gather.6
